TPU v7x, 32 devices: a whole 2x2x4 slice. The times are simulated.
32 devices in a mesh: mlong: 8 (over y, x, core), mshort: 4 (over z).
Axes of the slice: x: 2, y: 2, z: 4, core: 2. Of those that a mesh axis runs over, the one named last changes fastest.
Arguments:
- acq_traces: bfloat16 [16384, 1024], P(('mlong', 'mshort')), may hold values from -6 to 6
- route_owner: int32 [16384], P(('mlong', 'mshort')), may hold values from -1 to 31, as said below
- route_row: int32 [16384], P(('mlong', 'mshort')), may hold values from -1 to 511, as said below
- route_fold: int32 [16384], P(('mlong', 'mshort')), may hold values from 0 to 3
- sample_bits: int32 [16384, 64], P(('mlong', 'mshort')), may hold values from 0 to 65535
- left_factors: bfloat16 [16384, 4, 128], P(('mlong', 'mshort')), may hold values from -0.5 to 0.5
- right_factors: bfloat16 [4, 32768, 128], P(None, ('mlong', 'mshort')), may hold values from -6 to 6
Outputs:
- new_right: float32 [4, 32768, 128], P(None, ('mlong', 'mshort'))
- trace_residuals: bfloat16 [16384, 1024], P(('mlong', 'mshort'))
Inputs may be any that keep to these rules, and one draw needn't show every extreme that they name: route_owner: -1 marks an empty slot. In each device's 16 * 32 slots no owner is named more than 16 times; some owner is named exactly 16 times in every device's slots. Every owner is named somewhere. route_row: -1 exactly where route_owner is -1. No pair (route_owner, route_row) occurs twice.
All inputs are finite; a program needn't handle non-finite values.
Results may differ from a plain program's by a relative error of at most 0.0036.
Values may be sent and summed in bfloat16 or wider, within the bound.
A program may use at most 64 MiB of HBM per device.

v0:
```python
import functools

import jax
import jax.numpy as jnp
from jax import lax
from jax.experimental import pallas as pl
from jax.experimental.pallas import tpu as pltpu
from jax.sharding import PartitionSpec as P

RANK = 128
FOLDS = 4
H = 4
CX = 16
CY = 32


def padded(x, sides, width):
    for axis, dim in sides:
        count, length = (lax.axis_size(axis), x.shape[dim])
        up = [(i, (i + 1) % count) for i in range(count - 1)]
        down = [(j, i) for i, j in up]
        last = lax.slice_in_dim(x, length - width, length, axis=dim)
        initial = lax.slice_in_dim(x, 0, width, axis=dim)
        before = lax.ppermute(last, axis, up)
        after = lax.ppermute(initial, axis, down)
        x = jnp.concatenate([before, x, after], axis=dim)
    return x


def unpack(bits):
    shifts = jnp.arange(16, dtype=jnp.int32)
    flags = jnp.bitwise_and(lax.shift_right_logical(bits[:, :, None], shifts[None, None, :]), 1)
    return flags.reshape(bits.shape[0], -1).astype(jnp.float32)


def chol_right(cross, gram):
    chol = jnp.linalg.cholesky(gram)
    first = lax.linalg.triangular_solve(chol, cross, left_side=False, lower=True, transpose_a=True)
    return lax.linalg.triangular_solve(chol, first, left_side=False, lower=True, transpose_a=False)


def local(acq_traces, route_owner, route_row, route_fold, sample_bits, left_factors, right_factors):
    n_long = lax.axis_size("mlong")
    n_short = lax.axis_size("mshort")
    peers = n_long * n_short
    rows = acq_traces.shape[0]
    width = acq_traces.shape[1]
    cap = rows // peers
    total = peers * cap
    grid_bits = sample_bits.reshape(CX, CY, width // 16)
    grid_left = left_factors.reshape(CX, CY, FOLDS * RANK)
    valid = route_owner >= 0
    owner = jnp.where(valid, route_owner, 0)
    onehot = (
        (owner[:, None] == jnp.arange(peers, dtype=jnp.int32)[None, :]) & valid[:, None]
    ).astype(jnp.int32)
    within = jnp.sum(jnp.cumsum(onehot, axis=0) * onehot, axis=1) - 1
    place = jnp.where(valid, owner * cap + within, total)
    source = (
        jnp.full((total,), rows, jnp.int32)
        .at[place]
        .set(jnp.arange(rows, dtype=jnp.int32), mode="drop")
    )
    filled_slot = source < rows
    pick = jnp.minimum(source, rows - 1)
    send_traces = jnp.where(
        filled_slot[:, None], jnp.take(acq_traces, pick, axis=0), jnp.zeros((), jnp.bfloat16)
    )
    send_rows = jnp.where(filled_slot, jnp.take(route_row, pick), -1)
    send_folds = jnp.where(filled_slot, jnp.take(route_fold, pick), -1)
    got_traces, got_rows, got_folds = (
        lax.all_to_all(send_traces, ("mlong", "mshort"), split_axis=0, concat_axis=0, tiled=True),
        lax.all_to_all(send_rows, ("mlong", "mshort"), split_axis=0, concat_axis=0, tiled=True),
        lax.all_to_all(send_folds, ("mlong", "mshort"), split_axis=0, concat_axis=0, tiled=True),
    )
    arrival = (
        jnp.full((rows,), total, jnp.int32)
        .at[jnp.where(got_rows >= 0, got_rows, rows)]
        .set(jnp.arange(total, dtype=jnp.int32), mode="drop")
    )
    present = arrival < total
    slot_at = jnp.minimum(arrival, total - 1)
    data = jnp.where(
        present[:, None], jnp.take(got_traces, slot_at, axis=0), jnp.zeros((), jnp.bfloat16)
    )
    fold = jnp.where(present, jnp.take(got_folds, slot_at), -1)
    wide_data, wide_bits, wide_fold, wide_left = (
        padded(data.reshape(CX, CY, width), (("mlong", 0), ("mshort", 1)), H),
        padded(grid_bits, (("mlong", 0), ("mshort", 1)), H),
        padded(fold.reshape(CX, CY), (("mlong", 0), ("mshort", 1)), H),
        padded(grid_left, (("mlong", 0), ("mshort", 1)), H),
    )
    d_win = wide_data.reshape(-1, width)
    f_win = wide_fold.reshape(-1)
    l_win = wide_left.reshape(-1, FOLDS, RANK)
    seen = unpack(wide_bits.reshape(-1, width // 16)) * (f_win >= 0)[:, None].astype(jnp.float32)
    s_core = unpack(sample_bits) * (fold >= 0)[:, None].astype(jnp.float32)
    ridge = jnp.eye(RANK, dtype=jnp.float32)
    updates = []
    chosen = jnp.zeros((rows, width), jnp.float32)
    for f in range(FOLDS):
        factor = l_win[:, f]
        pred = jnp.dot(factor, right_factors[f].T, preferred_element_type=jnp.float32)
        train = seen * (f_win != f)[:, None].astype(jnp.float32)
        imputed = (train * d_win.astype(jnp.float32) + (1.0 - train) * pred).astype(jnp.bfloat16)
        cross = jnp.dot(imputed.T, factor, preferred_element_type=jnp.float32)
        gram = jnp.dot(factor.T, factor, preferred_element_type=jnp.float32) + ridge
        update = chol_right(cross, gram)
        updates.append(update)
        core_pred = jnp.dot(
            left_factors[:, f], update.astype(jnp.bfloat16).T, preferred_element_type=jnp.float32
        )
        chosen = chosen + (fold == f)[:, None].astype(jnp.float32) * core_pred
    new_right = jnp.stack(updates)
    resid = (s_core * (data.astype(jnp.float32) - chosen)).astype(jnp.bfloat16)
    back = jnp.where(
        (got_rows >= 0)[:, None],
        jnp.take(resid, jnp.maximum(got_rows, 0), axis=0),
        jnp.zeros((), jnp.bfloat16),
    )
    returned = lax.all_to_all(back, ("mlong", "mshort"), split_axis=0, concat_axis=0, tiled=True)
    trace_residuals = jnp.where(
        valid[:, None],
        jnp.take(returned, jnp.minimum(place, total - 1), axis=0),
        jnp.zeros((), jnp.bfloat16),
    )
    return (new_right, trace_residuals)


MESH = pl.DeviceIdType.MESH
WIN = 1024
CORE = CX * CY
WIDE = FOLDS * RANK
NT = (((1,), (1,)), ((), ()))
HALO = (
    (1, 0, False, CORE - H * CY, CORE, H * CY),
    (-1, 0, False, 0, CORE + H * CY, H * CY),
    (0, 1, True, H * CX, CORE + 2 * H * CY, H * CX),
    (0, -1, True, 0, CORE + 2 * H * CY + H * CX, H * CX),
    (1, 1, True, 2 * H * CX + 48, CORE + 2 * H * (CX + CY), 16),
    (1, -1, True, 2 * H * CX + 32, CORE + 2 * H * (CX + CY) + 16, 16),
    (-1, 1, True, 2 * H * CX + 16, CORE + 2 * H * (CX + CY) + 32, 16),
    (-1, -1, True, 2 * H * CX, CORE + 2 * H * (CX + CY) + 48, 16),
)
PACK = 2 * H * CX + 64


def iota(shape, dim):
    return lax.broadcasted_iota(jnp.int32, shape, dim)


def flags(mask, dtype=jnp.bfloat16):
    return jnp.where(mask, 1.0, 0.0).astype(dtype)


def dot(a, b, dims=(((1,), (0,)), ((), ())), precision=None):
    return lax.dot_general(a, b, dims, precision=precision, preferred_element_type=jnp.float32)


def packed_rows(shape):
    t = iota(shape, 0)
    u = t - 2 * H * CX
    side = jnp.where(t < H * CX, 0, CY - H)
    v = jnp.where(t < H * CX, t, t - H * CX)
    edge = (v // H) * CY + v % H + side
    k = u // 16
    w = u % 16
    corner = (w // H + jnp.where(k >= 2, CX - H, 0)) * CY + w % H + jnp.where(k % 2 == 1, CY - H, 0)
    return jnp.where(u < 0, edge, corner)


def kernel(
    n_long, n_short, traces, own, row, fold, side, right, news, out,
    lw, lpack, dw, dpack, meta_out, meta_in, send, got, ret, back, pred, seen, cross, lt, gram, vmat, qmat, resid, newb,
    meta_s, meta_r, data_s, data_r, ret_s, ret_r, hl_s, hl_r, hd_s, hd_r,
):
    peers = n_long * n_short
    cap = CORE // peers
    a = lax.axis_index("mlong")
    c = lax.axis_index("mshort")
    me = a * n_short + c
    width = traces.shape[1]

    lw[0:CORE, :] = side[...]
    lw[CORE:WIN, :] = jnp.zeros((WIN - CORE, WIDE + 128), jnp.bfloat16)
    dw[CORE:WIN, width : width + 128] = jnp.zeros((WIN - CORE, 128), jnp.bfloat16)

    barrier = pltpu.get_barrier_semaphore()

    def greet(k, carry):
        q = lax.rem(me + k, peers)
        pl.semaphore_signal(barrier, inc=1, device_id=(q // n_short, lax.rem(q, n_short)), device_id_type=MESH)
        return carry

    lax.fori_loop(1, peers, greet, 0)

    pick = flags(packed_rows((PACK, CORE)) == iota((PACK, CORE), 1))
    lpack[...] = dot(pick, side[...]).astype(jnp.bfloat16)

    owner = own[...]
    oh = flags(iota((peers, CORE), 0) == owner, jnp.float32)
    tri = flags(iota((CORE, CORE), 0) < iota((CORE, CORE), 1))
    cum = dot(oh.astype(jnp.bfloat16), tri)
    within = jnp.sum(oh * cum, axis=0, keepdims=True).astype(jnp.int32)
    place = jnp.where(owner >= 0, owner * cap + within, -1)
    rows = row[...]
    vals = [(rows // 128).astype(jnp.float32), (rows % 128).astype(jnp.float32), (fold[...] + 1).astype(jnp.float32)]
    left = jnp.concatenate([oh * v for v in vals], axis=1).astype(jnp.bfloat16)
    rightm = jnp.concatenate([flags(iota((128, CORE), 0) == within + 32 * i) for i in range(3)], axis=1)
    meta = dot(left, rightm, NT)
    for p in range(peers):
        meta_out[p] = meta[p : p + 1, :]
    meta_in[me] = meta_out[me]

    pl.semaphore_wait(barrier, peers - 1)

    def halo(buffer, pack, send_sem, recv_sem, i):
        da, dc, packed, start, dst, count = HALO[i]
        here = pack if packed else buffer
        return pltpu.make_async_remote_copy(
            src_ref=here.at[pl.ds(start, count)],
            dst_ref=buffer.at[pl.ds(dst, count)],
            send_sem=send_sem.at[i],
            recv_sem=recv_sem.at[i],
            device_id=(a + da, c + dc),
            device_id_type=MESH,
        )

    def inside(da, dc):
        return (a + da >= 0) & (a + da < n_long) & (c + dc >= 0) & (c + dc < n_short)

    def halo_start(*refs):
        for i in range(8):
            @pl.when(inside(HALO[i][0], HALO[i][1]))
            def _():
                halo(*refs, i).start()

    def halo_recv(*refs):
        for i in range(8):
            @pl.when(inside(-HALO[i][0], -HALO[i][1]))
            def _():
                halo(*refs, i).wait_recv()

    def halo_sent(*refs):
        for i in range(8):
            @pl.when(inside(HALO[i][0], HALO[i][1]))
            def _():
                halo(*refs, i).wait_send()

    def swap(src, dst, send_sem, recv_sem, k):
        to = lax.rem(me + k, peers)
        return pltpu.make_async_remote_copy(
            src_ref=src.at[to],
            dst_ref=dst.at[me],
            send_sem=send_sem.at[k],
            recv_sem=recv_sem.at[k],
            device_id=(to // n_short, lax.rem(to, n_short)),
            device_id_type=MESH,
        )

    def arriving(src, dst, send_sem, recv_sem, k):
        origin = lax.rem(me + peers - k, peers)
        return pltpu.make_async_remote_copy(
            src_ref=src.at[origin],
            dst_ref=dst.at[origin],
            send_sem=send_sem.at[k],
            recv_sem=recv_sem.at[k],
            device_id=(origin // n_short, lax.rem(origin, n_short)),
            device_id_type=MESH,
        )

    def swap_start(*refs):
        def go(k, carry):
            swap(*refs, k).start()
            return carry

        lax.fori_loop(1, peers, go, 0)

    def swap_recv(*refs):
        def go(k, carry):
            arriving(*refs, k).wait_recv()
            return carry

        lax.fori_loop(1, peers, go, 0)

    def swap_sent(*refs):
        def go(k, carry):
            swap(*refs, k).wait_send()
            return carry

        lax.fori_loop(1, peers, go, 0)

    metas = (meta_out, meta_in, meta_s, meta_r)
    datas = (send, got, data_s, data_r)
    rets = (back, ret, ret_s, ret_r)
    lefts = (lw, lpack, hl_s, hl_r)
    halos = (dw, dpack, hd_s, hd_r)
    halo_start(*lefts)
    swap_start(*metas)

    def spread(t, carry):
        take = flags(iota((128, CORE), 0) + t * 128 == place)
        block = dot(take, traces[...]).astype(jnp.bfloat16)
        send[pl.ds(t * (128 // cap), 128 // cap)] = block.reshape(128 // cap, cap, width)
        return carry

    lax.fori_loop(0, CORE // 128, spread, 0)
    got[me] = send[me]
    swap_start(*datas)

    eye = iota((CORE, CORE), 0) == iota((CORE, CORE), 1)

    def column(line):
        return jnp.sum(jnp.where(eye, line.astype(jnp.float32), 0.0), axis=1, keepdims=True).astype(jnp.int32)

    qmat[...] = flags(column(place) == iota((CORE, CORE), 1))

    halo_recv(*lefts)
    for f in range(FOLDS):
        factor = lw[:, f * RANK : (f + 1) * RANK]
        lt[f] = factor.T
        ident = flags(iota((RANK, RANK), 0) == iota((RANK, RANK), 1), jnp.float32)
        gram[f] = dot(lt[f], factor) + ident

    def eliminate(b, carry):
        k0 = pl.multiple_of(b * 8, 8)
        panel = gram[:, pl.ds(k0, 8), :]
        first = panel
        lane = iota((FOLDS, 8, RANK), 2)
        sub = iota((FOLDS, 8, RANK), 1)
        for j in range(8):
            col = jnp.sum(jnp.where(lane == k0 + j, panel, 0.0), axis=2, keepdims=True)
            inv = 1.0 / col[:, j : j + 1, :]
            w = jnp.where(lane[:, 0:1, :] == k0 + j, inv, panel[:, j : j + 1, :] * inv)
            panel = jnp.where(sub == j, w, jnp.where(lane == k0 + j, 0.0, panel) - col * w)
        signed = jnp.where(lane < k0, -first, first)
        cols = iota((RANK, RANK), 1)
        for f in range(FOLDS):
            change = dot(signed[f].T, panel[f], precision=lax.Precision.HIGHEST)
            gram[f] = jnp.where((cols >= k0) & (cols < k0 + 8), 0.0, gram[f]) - change
        gram[:, pl.ds(k0, 8), :] = panel
        return carry

    lax.fori_loop(0, RANK // 8, eliminate, 0)

    words = iota((128, width), 0)
    offs = iota((128, width), 1)
    expand = flags(words == offs // 16 + jnp.where(offs % 16 >= 8, 64, 0))

    def masks(t, carry):
        r = pl.ds(pl.multiple_of(t * 128, 128), 128)
        byte = dot(lw[r, WIDE : WIDE + 128], expand).astype(jnp.int32)
        bit = lax.shift_right_logical(byte, iota((128, width), 1) % 8) & 1
        seen[r, :] = bit.astype(jnp.float32).astype(jnp.bfloat16)
        return carry

    lax.fori_loop(0, WIN // 128, masks, 0)

    for f in range(FOLDS):
        def predict(t, carry, f=f):
            r = pl.ds(pl.multiple_of(t * 128, 128), 128)
            pred[f, r, :] = dot(lw[r, f * RANK : (f + 1) * RANK], right[f], NT).astype(jnp.bfloat16)
            return carry

        lax.fori_loop(0, WIN // 128, predict, 0)

    swap_recv(*metas)
    meta_got = meta_in[:, 0, :].astype(jnp.bfloat16)
    mine = iota((peers, CORE), 0) == iota((peers, CORE), 1) // cap
    lines = []
    for i in range(3):
        place_of = flags(iota((128, CORE), 0) == iota((128, CORE), 1) % cap + 32 * i)
        lines.append(jnp.sum(jnp.where(mine, dot(meta_got, place_of), 0.0), axis=0, keepdims=True))
    got_row = jnp.where(lines[2] > 0.5, lines[0] * 128.0 + lines[1], -1.0).astype(jnp.int32)
    got_fold = jnp.broadcast_to(lines[2], (128, CORE)).astype(jnp.bfloat16)
    vmat[...] = flags(column(got_row) == iota((CORE, CORE), 1))

    swap_recv(*datas)
    arrived = got[...].reshape(CORE, width)

    take = flags(packed_rows((PACK, CORE)) == got_row)
    dpack[:, 0:width] = dot(take, arrived).astype(jnp.bfloat16)
    dpack[:, width : width + 128] = dot(take, got_fold, NT).astype(jnp.bfloat16)

    def gather(t, carry):
        r = pl.ds(pl.multiple_of(t * 128, 128), 128)
        take = flags(iota((128, CORE), 0) + t * 128 == got_row)
        dw[r, 0:width] = dot(take, got[...].reshape(CORE, width)).astype(jnp.bfloat16)
        dw[r, width : width + 128] = dot(take, got_fold, NT).astype(jnp.bfloat16)
        return carry

    lax.fori_loop(0, CORE // 128, gather, 0)
    halo_start(*halos)

    cross[...] = jnp.zeros_like(cross)

    def accumulate(t):
        r = pl.ds(t * 256, 256)
        kind = jnp.concatenate([dw[r, width : width + 128]] * (width // 128), axis=1) * seen[r, :]
        values = dw[r, 0:width]
        for f in range(FOLDS):
            train = (kind > 0.5) & (kind != f + 1.0)
            filled = jnp.where(train, values, pred[f, r, :])
            cross[f] += dot(lt[f, :, t * 256 : (t + 1) * 256], filled)

    accumulate(0)
    accumulate(1)
    halo_recv(*halos)
    accumulate(2)
    accumulate(3)

    for f in range(FOLDS):
        update = dot(gram[f], cross[f], precision=lax.Precision.HIGHEST)
        cross[f] = update
        newb[f * RANK : (f + 1) * RANK, :] = update.astype(jnp.bfloat16)

    def residual(t, carry):
        r = pl.ds(pl.multiple_of(t * 128, 128), 128)
        kind = dw[r, width : width + 128]
        zero = jnp.zeros((128, RANK), jnp.bfloat16)
        chosen_left = jnp.concatenate(
            [jnp.where(kind == f + 1.0, lw[r, f * RANK : (f + 1) * RANK], zero) for f in range(FOLDS)], axis=1
        )
        chosen = dot(chosen_left, newb[...])
        live = jnp.concatenate([kind] * (width // 128), axis=1) * seen[r, :]
        diff = dw[r, 0:width].astype(jnp.float32) - chosen
        resid[r, :] = jnp.where(live.astype(jnp.float32) > 0.5, diff, 0.0).astype(jnp.bfloat16)
        return carry

    lax.fori_loop(0, CORE // 128, residual, 0)

    def send_back(t, carry):
        r = pl.ds(pl.multiple_of(t * 128, 128), 128)
        block = dot(vmat[r, :], resid[...]).astype(jnp.bfloat16)
        back[pl.ds(t * (128 // cap), 128 // cap)] = block.reshape(128 // cap, cap, width)
        return carry

    lax.fori_loop(0, CORE // 128, send_back, 0)
    ret[me] = back[me]
    swap_start(*rets)

    for f in range(FOLDS):
        news[f] = cross[f].T

    swap_recv(*rets)

    def deliver(t, carry):
        r = pl.ds(pl.multiple_of(t * 128, 128), 128)
        out[r, :] = dot(qmat[r, :], ret[...].reshape(CORE, width)).astype(jnp.bfloat16)
        return carry

    lax.fori_loop(0, CORE // 128, deliver, 0)

    swap_sent(*metas)
    swap_sent(*datas)
    swap_sent(*rets)
    halo_sent(*lefts)
    halo_sent(*halos)


def fused(acq_traces, route_owner, route_row, route_fold, sample_bits, left_factors, right_factors):
    n_long = lax.axis_size("mlong")
    n_short = lax.axis_size("mshort")
    peers = n_long * n_short
    rows, width = acq_traces.shape
    cap = rows // peers
    low = jnp.bitwise_and(sample_bits, 255).astype(jnp.bfloat16)
    high = lax.shift_right_logical(sample_bits, 8).astype(jnp.bfloat16)
    side = jnp.concatenate([left_factors.reshape(rows, WIDE), low, high], axis=1)
    vmem = pl.BlockSpec(memory_space=pltpu.VMEM)
    bf = jnp.bfloat16
    dma = pltpu.SemaphoreType.DMA
    return pl.pallas_call(
        functools.partial(kernel, n_long, n_short),
        out_shape=(
            jax.ShapeDtypeStruct((FOLDS, width, RANK), jnp.float32),
            jax.ShapeDtypeStruct((rows, width), bf),
        ),
        in_specs=[vmem] * 6,
        out_specs=(vmem, vmem),
        scratch_shapes=[
            pltpu.VMEM((WIN, WIDE + 128), bf),
            pltpu.VMEM((PACK, WIDE + 128), bf),
            pltpu.VMEM((WIN, width + 128), bf),
            pltpu.VMEM((PACK, width + 128), bf),
            pltpu.VMEM((peers, 1, 128), jnp.float32),
            pltpu.VMEM((peers, 1, 128), jnp.float32),
            pltpu.VMEM((peers, cap, width), bf),
            pltpu.VMEM((peers, cap, width), bf),
            pltpu.VMEM((peers, cap, width), bf),
            pltpu.VMEM((peers, cap, width), bf),
            pltpu.VMEM((FOLDS, WIN, width), bf),
            pltpu.VMEM((WIN, width), bf),
            pltpu.VMEM((FOLDS, RANK, width), jnp.float32),
            pltpu.VMEM((FOLDS, RANK, WIN), bf),
            pltpu.VMEM((FOLDS, RANK, RANK), jnp.float32),
            pltpu.VMEM((CORE, CORE), bf),
            pltpu.VMEM((CORE, CORE), bf),
            pltpu.VMEM((CORE, width), bf),
            pltpu.VMEM((WIDE, width), bf),
            dma((peers,)), dma((peers,)), dma((peers,)), dma((peers,)), dma((peers,)), dma((peers,)),
            dma((8,)), dma((8,)), dma((8,)), dma((8,)),
        ],
        compiler_params=pltpu.CompilerParams(
            collective_id=0, has_side_effects=True, vmem_limit_bytes=56 * 1024 * 1024
        ),
    )(
        acq_traces, route_owner.reshape(1, rows), route_row.reshape(1, rows), route_fold.reshape(1, rows),
        side, right_factors,
    )


def solution(mesh):
    in_specs = (
        P(("mlong", "mshort"), None),
        P(("mlong", "mshort")),
        P(("mlong", "mshort")),
        P(("mlong", "mshort")),
        P(("mlong", "mshort"), None),
        P(("mlong", "mshort"), None, None),
        P(None, ("mlong", "mshort"), None),
    )
    out_specs = (P(None, ("mlong", "mshort"), None), P(("mlong", "mshort"), None))
    peers = mesh.shape["mlong"] * mesh.shape["mshort"]
    body = fused if peers * 16 == CX * CY else local
    return jax.shard_map(body, mesh=mesh, in_specs=in_specs, out_specs=out_specs, check_vma=False)
```

profile of v0, /device:TPU:0, one launch (start us, length us, event | category | flops | bytes accessed | tf_op | source)
XLA Modules:
  0.0 93.9 jit_solution(9046592121151672529)
XLA Ops:
  0.6 1.0 %copy.11 = s32[512,64]{1,0:T(8,128)S(1)} copy(s32[512,64]{0,1:T(8,128)} %param.11) | data formatting | bytes 262144 | tf_op args[4]
  1.7 0.1 and_convert_fusion
  1.7 1.1 %copy.17 = bf16[64,8,4,128]{3,1,2,0:T(8,128)(2,1)S(1)} copy(bf16[64,8,4,128]{3,2,1,0:T(4,128)(2,1)} %bitcast.8) | data formatting | bytes 1048576
  2.9 0.9 %pad_maximum_fusion.side = bf16[512,640]{1,0:T(8,128)(2,1)} fusion(bf16[512,64]{1,0:T(8,128)(2,1)S(1)} %get-tuple-element.3, bf16[512,64]{1,0:T(8,128)(2,1)S(1)} %get-tuple-element.2, bf16[512,512]{1,0:T(8,128)(2,1)S(1)} %bitcast.7), kind=kLoop, calls=%fused_computation | loop fusion | flops 1966080 | bytes 1310720 | tf_op jit(solution)/shard_map/concatenate | solution.py:469
  3.8 86.0 %shard_map.86 = (f32[4,1024,128]{2,1,0:T(8,128)}, bf16[512,1024]{1,0:T(8,128)(2,1)}) custom-call(bf16[512,1024]{1,0:T(8,128)(2,1)} %traces.1, s32[1,512]{1,0:T(1,128)} %bitcast.9, s32[1,512]{1,0:T(1,128)} %bitcast.10, s32[1,512]{1,0:T(1,128)} %bitcast.11, bf16[512,640]{1,0:T(8,128)(2,1)} %pad_maximum_fusion.side, bf16[4,1024,128]{2,1,0:T(8,128)(2,1)} %right.1), custom_call_target="tpu_custom_call" | custom-call | tf_op jit(solution)/shard_map/pallas_call | solution.py:473
  89.8 0.0 copy-start
  89.8 3.1 %copy.20 = f32[4,1024,128]{2,1,0:T(8,128)} copy(f32[4,1024,128]{2,1,0:T(8,128)} %get-tuple-element.6) | data formatting | bytes 4194304
  92.9 0.0 copy-done
  92.9 1.0 %copy.21 = bf16[512,1024]{1,0:T(8,128)(2,1)} copy(bf16[512,1024]{1,0:T(8,128)(2,1)S(1)} %copy-done) | data formatting | bytes 2097152
Async XLA Ops:
  89.8 3.1 %copy-start = (bf16[512,1024]{1,0:T(8,128)(2,1)S(1)}, bf16[512,1024]{1,0:T(8,128)(2,1)}, u32[]{:S(2)}) copy-start(bf16[512,1024]{1,0:T(8,128)(2,1)} %get-tuple-element.7) | copy-start | bytes 3145732
where the time goes:
time: 94.3 us; the launch traced here: 93.9 us
  Pallas kernels  86 us (91%)
  local copies, waits for them, and re-layouts  6.26 us (7%)
  other arithmetic  1 us (1%)
    pallas_call x1, Pallas kernels, fused(): pl.pallas_call(functools.partial(kernel, n_long, n_short), out_shape=(jax...  86 us
    unnamed x6, local copies, waits for them, and re-layouts  6.26 us

commit v1 on v0

--- a/solution.py
+++ b/solution.py
@@ -131,6 +131,7 @@
 WIN = 1024
 CORE = CX * CY
 WIDE = FOLDS * RANK
+PARTS = 4
 NT = (((1,), (1,)), ((), ()))
 HALO = (
     (1, 0, False, CORE - H * CY, CORE, H * CY),
@@ -171,8 +172,8 @@
 
 def kernel(
     n_long, n_short, traces, own, row, fold, side, right, news, out,
-    lw, lpack, dw, dpack, meta_out, meta_in, send, got, ret, back, pred, seen, cross, lt, gram, vmat, qmat, resid, newb,
-    meta_s, meta_r, data_s, data_r, ret_s, ret_r, hl_s, hl_r, hd_s, hd_r,
+    lw, lpack, fw, fpack, dw, dpack, meta_out, meta_in, send, got, ret, back, pred, kind, cross, lt, gram, umat, vmat, qmat, csel,
+    meta_s, meta_r, data_s, data_r, ret_s, ret_r, hl_s, hl_r, hf_s, hf_r, hd_s, hd_r,
 ):
     peers = n_long * n_short
     cap = CORE // peers
@@ -183,7 +184,9 @@
 
     lw[0:CORE, :] = side[...]
     lw[CORE:WIN, :] = jnp.zeros((WIN - CORE, WIDE + 128), jnp.bfloat16)
-    dw[CORE:WIN, width : width + 128] = jnp.zeros((WIN - CORE, 128), jnp.bfloat16)
+    fw[CORE:WIN, :] = jnp.zeros((WIN - CORE, 128), jnp.bfloat16)
+    dw[CORE:WIN, :] = jnp.zeros((WIN - CORE, width), jnp.bfloat16)
+    part = width // PARTS
 
     barrier = pltpu.get_barrier_semaphore()
 
@@ -214,14 +217,14 @@
 
     pl.semaphore_wait(barrier, peers - 1)
 
-    def halo(buffer, pack, send_sem, recv_sem, i):
+    def halo(buffer, pack, send_sem, recv_sem, at, span, i):
         da, dc, packed, start, dst, count = HALO[i]
         here = pack if packed else buffer
         return pltpu.make_async_remote_copy(
-            src_ref=here.at[pl.ds(start, count)],
-            dst_ref=buffer.at[pl.ds(dst, count)],
-            send_sem=send_sem.at[i],
-            recv_sem=recv_sem.at[i],
+            src_ref=here.at[pl.ds(start, count), pl.ds(at * span, span)],
+            dst_ref=buffer.at[pl.ds(dst, count), pl.ds(at * span, span)],
+            send_sem=send_sem.at[at, i],
+            recv_sem=recv_sem.at[at, i],
             device_id=(a + da, c + dc),
             device_id_type=MESH,
         )
@@ -247,24 +250,24 @@
             def _():
                 halo(*refs, i).wait_send()
 
-    def swap(src, dst, send_sem, recv_sem, k):
+    def swap(src, dst, send_sem, recv_sem, at, span, k):
         to = lax.rem(me + k, peers)
         return pltpu.make_async_remote_copy(
-            src_ref=src.at[to],
-            dst_ref=dst.at[me],
-            send_sem=send_sem.at[k],
-            recv_sem=recv_sem.at[k],
+            src_ref=src.at[to, :, pl.ds(at * span, span)],
+            dst_ref=dst.at[me, :, pl.ds(at * span, span)],
+            send_sem=send_sem.at[at, k],
+            recv_sem=recv_sem.at[at, k],
             device_id=(to // n_short, lax.rem(to, n_short)),
             device_id_type=MESH,
         )
 
-    def arriving(src, dst, send_sem, recv_sem, k):
+    def arriving(src, dst, send_sem, recv_sem, at, span, k):
         origin = lax.rem(me + peers - k, peers)
         return pltpu.make_async_remote_copy(
-            src_ref=src.at[origin],
-            dst_ref=dst.at[origin],
-            send_sem=send_sem.at[k],
-            recv_sem=recv_sem.at[k],
+            src_ref=src.at[origin, :, pl.ds(at * span, span)],
+            dst_ref=dst.at[origin, :, pl.ds(at * span, span)],
+            send_sem=send_sem.at[at, k],
+            recv_sem=recv_sem.at[at, k],
             device_id=(origin // n_short, lax.rem(origin, n_short)),
             device_id_type=MESH,
         )
@@ -290,11 +293,12 @@
 
         lax.fori_loop(1, peers, go, 0)
 
-    metas = (meta_out, meta_in, meta_s, meta_r)
-    datas = (send, got, data_s, data_r)
-    rets = (back, ret, ret_s, ret_r)
-    lefts = (lw, lpack, hl_s, hl_r)
-    halos = (dw, dpack, hd_s, hd_r)
+    metas = (meta_out, meta_in, meta_s, meta_r, 0, 128)
+    datas = [(send, got, data_s, data_r, at, part) for at in range(PARTS)]
+    rets = [(back, ret, ret_s, ret_r, at, part) for at in range(PARTS)]
+    lefts = (lw, lpack, hl_s, hl_r, 0, WIDE + 128)
+    folds = (fw, fpack, hf_s, hf_r, 0, 128)
+    halos = [(dw, dpack, hd_s, hd_r, at, part) for at in range(PARTS)]
     halo_start(*lefts)
     swap_start(*metas)
 
@@ -306,7 +310,8 @@
 
     lax.fori_loop(0, CORE // 128, spread, 0)
     got[me] = send[me]
-    swap_start(*datas)
+    for at in range(PARTS):
+        swap_start(*datas[at])
 
     eye = iota((CORE, CORE), 0) == iota((CORE, CORE), 1)
 
@@ -314,6 +319,25 @@
         return jnp.sum(jnp.where(eye, line.astype(jnp.float32), 0.0), axis=1, keepdims=True).astype(jnp.int32)
 
     qmat[...] = flags(column(place) == iota((CORE, CORE), 1))
+
+    swap_recv(*metas)
+    meta_got = meta_in[:, 0, :].astype(jnp.bfloat16)
+    mine = iota((peers, CORE), 0) == iota((peers, CORE), 1) // cap
+    lines = []
+    for i in range(3):
+        place_of = flags(iota((128, CORE), 0) == iota((128, CORE), 1) % cap + 32 * i)
+        lines.append(jnp.sum(jnp.where(mine, dot(meta_got, place_of), 0.0), axis=0, keepdims=True))
+    got_row = jnp.where(lines[2] > 0.5, lines[0] * 128.0 + lines[1], -1.0).astype(jnp.int32)
+    got_fold = jnp.broadcast_to(lines[2], (128, CORE)).astype(jnp.bfloat16)
+    umat[0:CORE, :] = flags(iota((CORE, CORE), 0) == got_row)
+    umat[CORE : CORE + PACK, :] = flags(packed_rows((PACK, CORE)) == got_row)
+    fw[0:CORE, :] = dot(umat[0:CORE, :], got_fold, NT).astype(jnp.bfloat16)
+    fpack[...] = dot(umat[CORE : CORE + PACK, :], got_fold, NT).astype(jnp.bfloat16)
+    halo_start(*folds)
+    vmat[...] = flags(column(got_row) == iota((CORE, CORE), 1))
+    for f in range(FOLDS):
+        fs = slice(f * RANK, (f + 1) * RANK)
+        csel[:, fs] = jnp.where(fw[0:CORE, :] == f + 1.0, side[:, fs], jnp.zeros((CORE, RANK), jnp.bfloat16))
 
     halo_recv(*lefts)
     for f in range(FOLDS):
@@ -343,6 +367,7 @@
 
     lax.fori_loop(0, RANK // 8, eliminate, 0)
 
+    halo_recv(*folds)
     words = iota((128, width), 0)
     offs = iota((128, width), 1)
     expand = flags(words == offs // 16 + jnp.where(offs % 16 >= 8, 64, 0))
@@ -351,10 +376,52 @@
         r = pl.ds(pl.multiple_of(t * 128, 128), 128)
         byte = dot(lw[r, WIDE : WIDE + 128], expand).astype(jnp.int32)
         bit = lax.shift_right_logical(byte, iota((128, width), 1) % 8) & 1
-        seen[r, :] = bit.astype(jnp.float32).astype(jnp.bfloat16)
+        flag = bit.astype(jnp.float32).astype(jnp.bfloat16)
+        kind[r, :] = jnp.concatenate([fw[r, :]] * (width // 128), axis=1) * flag
         return carry
 
     lax.fori_loop(0, WIN // 128, masks, 0)
+
+    def collect(at):
+        swap_recv(*datas[at])
+        cols = slice(at * part, (at + 1) * part)
+
+        def gather(t, carry):
+            r = pl.ds(pl.multiple_of(t * 128, 128), 128)
+            dw[r, cols] = dot(umat[r, :], got[:, :, cols].reshape(CORE, part)).astype(jnp.bfloat16)
+            return carry
+
+        dpack[:, cols] = dot(umat[CORE : CORE + PACK, :], got[:, :, cols].reshape(CORE, part)).astype(jnp.bfloat16)
+        lax.fori_loop(0, CORE // 128, gather, 0)
+        halo_start(*halos[at])
+
+    def finish(at):
+        cols = slice(at * part, (at + 1) * part)
+        halo_recv(*halos[at])
+        newb = []
+        for f in range(FOLDS):
+            sort = kind[:, cols]
+            train = (sort > 0.5) & (sort != f + 1.0)
+            filled = jnp.where(train, dw[:, cols], pred[f, :, cols])
+            total = dot(lt[f], filled)
+            update = dot(gram[f], total, precision=lax.Precision.HIGHEST)
+            cross[f, :, cols] = update
+            newb.append(update.astype(jnp.bfloat16))
+        chosen = dot(csel[...], jnp.concatenate(newb, axis=0))
+        live = kind[0:CORE, cols].astype(jnp.float32) > 0.5
+        diff = dw[0:CORE, cols].astype(jnp.float32) - chosen
+        resid = jnp.where(live, diff, 0.0).astype(jnp.bfloat16)
+        block = dot(vmat[...], resid).astype(jnp.bfloat16)
+        back[:, :, cols] = block.reshape(peers, cap, part)
+        ret[me, :, cols] = back[me, :, cols]
+        swap_start(*rets[at])
+
+    def deliver(at):
+        cols = slice(at * part, (at + 1) * part)
+        swap_recv(*rets[at])
+        out[:, cols] = dot(qmat[...], ret[:, :, cols].reshape(CORE, part)).astype(jnp.bfloat16)
+
+    collect(0)
 
     for f in range(FOLDS):
         def predict(t, carry, f=f):
@@ -364,98 +431,25 @@
 
         lax.fori_loop(0, WIN // 128, predict, 0)
 
-    swap_recv(*metas)
-    meta_got = meta_in[:, 0, :].astype(jnp.bfloat16)
-    mine = iota((peers, CORE), 0) == iota((peers, CORE), 1) // cap
-    lines = []
-    for i in range(3):
-        place_of = flags(iota((128, CORE), 0) == iota((128, CORE), 1) % cap + 32 * i)
-        lines.append(jnp.sum(jnp.where(mine, dot(meta_got, place_of), 0.0), axis=0, keepdims=True))
-    got_row = jnp.where(lines[2] > 0.5, lines[0] * 128.0 + lines[1], -1.0).astype(jnp.int32)
-    got_fold = jnp.broadcast_to(lines[2], (128, CORE)).astype(jnp.bfloat16)
-    vmat[...] = flags(column(got_row) == iota((CORE, CORE), 1))
-
-    swap_recv(*datas)
-    arrived = got[...].reshape(CORE, width)
-
-    take = flags(packed_rows((PACK, CORE)) == got_row)
-    dpack[:, 0:width] = dot(take, arrived).astype(jnp.bfloat16)
-    dpack[:, width : width + 128] = dot(take, got_fold, NT).astype(jnp.bfloat16)
-
-    def gather(t, carry):
-        r = pl.ds(pl.multiple_of(t * 128, 128), 128)
-        take = flags(iota((128, CORE), 0) + t * 128 == got_row)
-        dw[r, 0:width] = dot(take, got[...].reshape(CORE, width)).astype(jnp.bfloat16)
-        dw[r, width : width + 128] = dot(take, got_fold, NT).astype(jnp.bfloat16)
-        return carry
-
-    lax.fori_loop(0, CORE // 128, gather, 0)
-    halo_start(*halos)
-
-    cross[...] = jnp.zeros_like(cross)
-
-    def accumulate(t):
-        r = pl.ds(t * 256, 256)
-        kind = jnp.concatenate([dw[r, width : width + 128]] * (width // 128), axis=1) * seen[r, :]
-        values = dw[r, 0:width]
-        for f in range(FOLDS):
-            train = (kind > 0.5) & (kind != f + 1.0)
-            filled = jnp.where(train, values, pred[f, r, :])
-            cross[f] += dot(lt[f, :, t * 256 : (t + 1) * 256], filled)
-
-    accumulate(0)
-    accumulate(1)
-    halo_recv(*halos)
-    accumulate(2)
-    accumulate(3)
-
-    for f in range(FOLDS):
-        update = dot(gram[f], cross[f], precision=lax.Precision.HIGHEST)
-        cross[f] = update
-        newb[f * RANK : (f + 1) * RANK, :] = update.astype(jnp.bfloat16)
-
-    def residual(t, carry):
-        r = pl.ds(pl.multiple_of(t * 128, 128), 128)
-        kind = dw[r, width : width + 128]
-        zero = jnp.zeros((128, RANK), jnp.bfloat16)
-        chosen_left = jnp.concatenate(
-            [jnp.where(kind == f + 1.0, lw[r, f * RANK : (f + 1) * RANK], zero) for f in range(FOLDS)], axis=1
-        )
-        chosen = dot(chosen_left, newb[...])
-        live = jnp.concatenate([kind] * (width // 128), axis=1) * seen[r, :]
-        diff = dw[r, 0:width].astype(jnp.float32) - chosen
-        resid[r, :] = jnp.where(live.astype(jnp.float32) > 0.5, diff, 0.0).astype(jnp.bfloat16)
-        return carry
-
-    lax.fori_loop(0, CORE // 128, residual, 0)
-
-    def send_back(t, carry):
-        r = pl.ds(pl.multiple_of(t * 128, 128), 128)
-        block = dot(vmat[r, :], resid[...]).astype(jnp.bfloat16)
-        back[pl.ds(t * (128 // cap), 128 // cap)] = block.reshape(128 // cap, cap, width)
-        return carry
-
-    lax.fori_loop(0, CORE // 128, send_back, 0)
-    ret[me] = back[me]
-    swap_start(*rets)
+    collect(1)
+    for at in range(PARTS):
+        finish(at)
+        if at + 2 < PARTS:
+            collect(at + 2)
 
     for f in range(FOLDS):
         news[f] = cross[f].T
 
-    swap_recv(*rets)
-
-    def deliver(t, carry):
-        r = pl.ds(pl.multiple_of(t * 128, 128), 128)
-        out[r, :] = dot(qmat[r, :], ret[...].reshape(CORE, width)).astype(jnp.bfloat16)
-        return carry
-
-    lax.fori_loop(0, CORE // 128, deliver, 0)
+    for at in range(PARTS):
+        deliver(at)
 
     swap_sent(*metas)
-    swap_sent(*datas)
-    swap_sent(*rets)
     halo_sent(*lefts)
-    halo_sent(*halos)
+    halo_sent(*folds)
+    for at in range(PARTS):
+        swap_sent(*datas[at])
+        swap_sent(*rets[at])
+        halo_sent(*halos[at])
 
 
 def fused(acq_traces, route_owner, route_row, route_fold, sample_bits, left_factors, right_factors):
@@ -481,8 +475,10 @@
         scratch_shapes=[
             pltpu.VMEM((WIN, WIDE + 128), bf),
             pltpu.VMEM((PACK, WIDE + 128), bf),
-            pltpu.VMEM((WIN, width + 128), bf),
-            pltpu.VMEM((PACK, width + 128), bf),
+            pltpu.VMEM((WIN, 128), bf),
+            pltpu.VMEM((PACK, 128), bf),
+            pltpu.VMEM((WIN, width), bf),
+            pltpu.VMEM((PACK, width), bf),
             pltpu.VMEM((peers, 1, 128), jnp.float32),
             pltpu.VMEM((peers, 1, 128), jnp.float32),
             pltpu.VMEM((peers, cap, width), bf),
@@ -494,12 +490,12 @@
             pltpu.VMEM((FOLDS, RANK, width), jnp.float32),
             pltpu.VMEM((FOLDS, RANK, WIN), bf),
             pltpu.VMEM((FOLDS, RANK, RANK), jnp.float32),
+            pltpu.VMEM((CORE + PACK, CORE), bf),
             pltpu.VMEM((CORE, CORE), bf),
             pltpu.VMEM((CORE, CORE), bf),
-            pltpu.VMEM((CORE, width), bf),
-            pltpu.VMEM((WIDE, width), bf),
-            dma((peers,)), dma((peers,)), dma((peers,)), dma((peers,)), dma((peers,)), dma((peers,)),
-            dma((8,)), dma((8,)), dma((8,)), dma((8,)),
+            pltpu.VMEM((CORE, WIDE), bf),
+            dma((1, peers)), dma((1, peers)), dma((PARTS, peers)), dma((PARTS, peers)), dma((PARTS, peers)), dma((PARTS, peers)),
+            dma((1, 8)), dma((1, 8)), dma((1, 8)), dma((1, 8)), dma((PARTS, 8)), dma((PARTS, 8)),
         ],
         compiler_params=pltpu.CompilerParams(
             collective_id=0, has_side_effects=True, vmem_limit_bytes=56 * 1024 * 1024

time: 94.3 us -> 96.5 us (1.023)
  Pallas kernels: 86 us -> 88.4 us
    pallas_call x1, Pallas kernels: 86 us -> 88.4 us  [fused(): pl.pallas_call(functools.partial(kernel, n_long, n_short), out_shape=(jax...]
where the time goes in v1:
time: 96.5 us; the launch traced here: 96.3 us
  Pallas kernels  88.4 us (92%)
  local copies, waits for them, and re-layouts  6.26 us (6%)
  other arithmetic  1 us (1%)
    pallas_call x1, Pallas kernels, fused(): pl.pallas_call(functools.partial(kernel, n_long, n_short), out_shape=(jax...  88.4 us
    unnamed x6, local copies, waits for them, and re-layouts  6.26 us

profile of v1, /device:TPU:0, one launch (start us, length us, event | category | flops | bytes accessed | tf_op | source)
XLA Modules:
  0.0 96.3 jit_solution(15613843064843075663)
XLA Ops:
  0.6 1.0 %copy.11 = s32[512,64]{1,0:T(8,128)S(1)} copy(s32[512,64]{0,1:T(8,128)} %param.11) | data formatting | bytes 262144 | tf_op args[4]
  1.7 0.1 and_convert_fusion
  1.7 1.1 %copy.17 = bf16[64,8,4,128]{3,1,2,0:T(8,128)(2,1)S(1)} copy(bf16[64,8,4,128]{3,2,1,0:T(4,128)(2,1)} %bitcast.8) | data formatting | bytes 1048576
  2.9 0.9 pad_maximum_fusion.side
  3.8 88.4 %shard_map.86 = (f32[4,1024,128]{2,1,0:T(8,128)}, bf16[512,1024]{1,0:T(8,128)(2,1)}) custom-call(bf16[512,1024]{1,0:T(8,128)(2,1)} %traces.1, s32[1,512]{1,0:T(1,128)} %bitcast.9, s32[1,512]{1,0:T(1,128)} %bitcast.10, s32[1,512]{1,0:T(1,128)} %bitcast.11, bf16[512,640]{1,0:T(8,128)(2,1)} %pad_maximum_fusion.side, bf16[4,1024,128]{2,1,0:T(8,128)(2,1)} %right.1), custom_call_target="tpu_custom_call" | custom-call | tf_op jit(solution)/shard_map/pallas_call | solution.py:467
  92.2 0.0 copy-start
  92.2 3.1 %copy.20 = f32[4,1024,128]{2,1,0:T(8,128)} copy(f32[4,1024,128]{2,1,0:T(8,128)} %get-tuple-element.6) | data formatting | bytes 4194304
  95.3 0.0 copy-done
  95.3 1.0 %copy.21 = bf16[512,1024]{1,0:T(8,128)(2,1)} copy(bf16[512,1024]{1,0:T(8,128)(2,1)S(1)} %copy-done) | data formatting | bytes 2097152
Async XLA Ops:
  92.2 3.1 %copy-start = (bf16[512,1024]{1,0:T(8,128)(2,1)S(1)}, bf16[512,1024]{1,0:T(8,128)(2,1)}, u32[]{:S(2)}) copy-start(bf16[512,1024]{1,0:T(8,128)(2,1)} %get-tuple-element.7) | copy-start | bytes 3145732

commit v2 on v1

--- a/solution.py
+++ b/solution.py
@@ -158,16 +158,30 @@
     return lax.dot_general(a, b, dims, precision=precision, preferred_element_type=jnp.float32)
 
 
+def div(x, n):
+    return lax.shift_right_arithmetic(x, n.bit_length() - 1)
+
+
+def mod(x, n):
+    return x & (n - 1)
+
+
 def packed_rows(shape):
     t = iota(shape, 0)
     u = t - 2 * H * CX
-    side = jnp.where(t < H * CX, 0, CY - H)
-    v = jnp.where(t < H * CX, t, t - H * CX)
-    edge = (v // H) * CY + v % H + side
-    k = u // 16
-    w = u % 16
-    corner = (w // H + jnp.where(k >= 2, CX - H, 0)) * CY + w % H + jnp.where(k % 2 == 1, CY - H, 0)
+    v = mod(t, H * CX)
+    edge = div(v, H) * CY + mod(v, H) + jnp.where(t < H * CX, 0, CY - H)
+    k = div(u, 16)
+    w = mod(u, 16)
+    corner = (div(w, H) + jnp.where(k >= 2, CX - H, 0)) * CY + mod(w, H) + jnp.where(mod(k, 2) == 1, CY - H, 0)
     return jnp.where(u < 0, edge, corner)
+
+
+def pieces(x):
+    top = x.astype(jnp.bfloat16).astype(jnp.float32)
+    rest = x - top
+    middle = rest.astype(jnp.bfloat16).astype(jnp.float32)
+    return top, middle, rest - middle
 
 
 def kernel(
@@ -197,9 +211,6 @@
 
     lax.fori_loop(1, peers, greet, 0)
 
-    pick = flags(packed_rows((PACK, CORE)) == iota((PACK, CORE), 1))
-    lpack[...] = dot(pick, side[...]).astype(jnp.bfloat16)
-
     owner = own[...]
     oh = flags(iota((peers, CORE), 0) == owner, jnp.float32)
     tri = flags(iota((CORE, CORE), 0) < iota((CORE, CORE), 1))
@@ -207,7 +218,7 @@
     within = jnp.sum(oh * cum, axis=0, keepdims=True).astype(jnp.int32)
     place = jnp.where(owner >= 0, owner * cap + within, -1)
     rows = row[...]
-    vals = [(rows // 128).astype(jnp.float32), (rows % 128).astype(jnp.float32), (fold[...] + 1).astype(jnp.float32)]
+    vals = [div(rows, 128).astype(jnp.float32), mod(rows, 128).astype(jnp.float32), (fold[...] + 1).astype(jnp.float32)]
     left = jnp.concatenate([oh * v for v in vals], axis=1).astype(jnp.bfloat16)
     rightm = jnp.concatenate([flags(iota((128, CORE), 0) == within + 32 * i) for i in range(3)], axis=1)
     meta = dot(left, rightm, NT)
@@ -255,20 +266,19 @@
         return pltpu.make_async_remote_copy(
             src_ref=src.at[to, :, pl.ds(at * span, span)],
             dst_ref=dst.at[me, :, pl.ds(at * span, span)],
-            send_sem=send_sem.at[at, k],
-            recv_sem=recv_sem.at[at, k],
+            send_sem=send_sem.at[at],
+            recv_sem=recv_sem.at[at],
             device_id=(to // n_short, lax.rem(to, n_short)),
             device_id_type=MESH,
         )
 
-    def arriving(src, dst, send_sem, recv_sem, at, span, k):
-        origin = lax.rem(me + peers - k, peers)
+    def all_of(src, dst, send_sem, recv_sem, at, span):
         return pltpu.make_async_remote_copy(
-            src_ref=src.at[origin, :, pl.ds(at * span, span)],
-            dst_ref=dst.at[origin, :, pl.ds(at * span, span)],
-            send_sem=send_sem.at[at, k],
-            recv_sem=recv_sem.at[at, k],
-            device_id=(origin // n_short, lax.rem(origin, n_short)),
+            src_ref=src.at[pl.ds(1, peers - 1), :, pl.ds(at * span, span)],
+            dst_ref=dst.at[pl.ds(1, peers - 1), :, pl.ds(at * span, span)],
+            send_sem=send_sem.at[at],
+            recv_sem=recv_sem.at[at],
+            device_id=(a, lax.rem(c + 1, n_short)),
             device_id_type=MESH,
         )
 
@@ -280,18 +290,10 @@
         lax.fori_loop(1, peers, go, 0)
 
     def swap_recv(*refs):
-        def go(k, carry):
-            arriving(*refs, k).wait_recv()
-            return carry
-
-        lax.fori_loop(1, peers, go, 0)
+        all_of(*refs).wait_recv()
 
     def swap_sent(*refs):
-        def go(k, carry):
-            swap(*refs, k).wait_send()
-            return carry
-
-        lax.fori_loop(1, peers, go, 0)
+        all_of(*refs).wait_send()
 
     metas = (meta_out, meta_in, meta_s, meta_r, 0, 128)
     datas = [(send, got, data_s, data_r, at, part) for at in range(PARTS)]
@@ -299,19 +301,18 @@
     lefts = (lw, lpack, hl_s, hl_r, 0, WIDE + 128)
     folds = (fw, fpack, hf_s, hf_r, 0, 128)
     halos = [(dw, dpack, hd_s, hd_r, at, part) for at in range(PARTS)]
+    swap_start(*metas)
+
+    take = flags(iota((CORE, CORE), 0) == place)
+    for at in range(PARTS):
+        cols = slice(at * part, (at + 1) * part)
+        send[:, :, cols] = dot(take, traces[:, cols]).astype(jnp.bfloat16).reshape(peers, cap, part)
+        swap_start(*datas[at])
+    got[me] = send[me]
+
+    pick = flags(packed_rows((PACK, CORE)) == iota((PACK, CORE), 1))
+    lpack[...] = dot(pick, side[...]).astype(jnp.bfloat16)
     halo_start(*lefts)
-    swap_start(*metas)
-
-    def spread(t, carry):
-        take = flags(iota((128, CORE), 0) + t * 128 == place)
-        block = dot(take, traces[...]).astype(jnp.bfloat16)
-        send[pl.ds(t * (128 // cap), 128 // cap)] = block.reshape(128 // cap, cap, width)
-        return carry
-
-    lax.fori_loop(0, CORE // 128, spread, 0)
-    got[me] = send[me]
-    for at in range(PARTS):
-        swap_start(*datas[at])
 
     eye = iota((CORE, CORE), 0) == iota((CORE, CORE), 1)
 
@@ -322,10 +323,10 @@
 
     swap_recv(*metas)
     meta_got = meta_in[:, 0, :].astype(jnp.bfloat16)
-    mine = iota((peers, CORE), 0) == iota((peers, CORE), 1) // cap
+    mine = iota((peers, CORE), 0) == div(iota((peers, CORE), 1), cap)
     lines = []
     for i in range(3):
-        place_of = flags(iota((128, CORE), 0) == iota((128, CORE), 1) % cap + 32 * i)
+        place_of = flags(iota((128, CORE), 0) == mod(iota((128, CORE), 1), cap) + 32 * i)
         lines.append(jnp.sum(jnp.where(mine, dot(meta_got, place_of), 0.0), axis=0, keepdims=True))
     got_row = jnp.where(lines[2] > 0.5, lines[0] * 128.0 + lines[1], -1.0).astype(jnp.int32)
     got_fold = jnp.broadcast_to(lines[2], (128, CORE)).astype(jnp.bfloat16)
@@ -346,53 +347,65 @@
         ident = flags(iota((RANK, RANK), 0) == iota((RANK, RANK), 1), jnp.float32)
         gram[f] = dot(lt[f], factor) + ident
 
-    def eliminate(b, carry):
-        k0 = pl.multiple_of(b * 8, 8)
-        panel = gram[:, pl.ds(k0, 8), :]
-        first = panel
-        lane = iota((FOLDS, 8, RANK), 2)
-        sub = iota((FOLDS, 8, RANK), 1)
-        for j in range(8):
-            col = jnp.sum(jnp.where(lane == k0 + j, panel, 0.0), axis=2, keepdims=True)
-            inv = 1.0 / col[:, j : j + 1, :]
-            w = jnp.where(lane[:, 0:1, :] == k0 + j, inv, panel[:, j : j + 1, :] * inv)
-            panel = jnp.where(sub == j, w, jnp.where(lane == k0 + j, 0.0, panel) - col * w)
-        signed = jnp.where(lane < k0, -first, first)
-        cols = iota((RANK, RANK), 1)
-        for f in range(FOLDS):
-            change = dot(signed[f].T, panel[f], precision=lax.Precision.HIGHEST)
-            gram[f] = jnp.where((cols >= k0) & (cols < k0 + 8), 0.0, gram[f]) - change
-        gram[:, pl.ds(k0, 8), :] = panel
-        return carry
-
-    lax.fori_loop(0, RANK // 8, eliminate, 0)
-
     halo_recv(*folds)
     words = iota((128, width), 0)
     offs = iota((128, width), 1)
-    expand = flags(words == offs // 16 + jnp.where(offs % 16 >= 8, 64, 0))
-
-    def masks(t, carry):
-        r = pl.ds(pl.multiple_of(t * 128, 128), 128)
+    expand = flags(words == div(offs, 16) + jnp.where(mod(offs, 16) >= 8, 64, 0))
+    steps = RANK // 8
+    tall = WIN // steps
+    quarter = FOLDS * WIN // steps
+
+    def eliminate(b, carry):
+        k0 = pl.multiple_of(b * 8, 8)
+        first = gram[:, pl.ds(k0, 8), :]
+        lane = iota((FOLDS, 8, RANK), 2)
+        sub = iota((FOLDS, 8, RANK), 1)
+        inner = (lane >= k0) & (lane < k0 + 8)
+        cols = [
+            jnp.broadcast_to(jnp.sum(jnp.where(lane == k0 + j, first, 0.0), axis=2, keepdims=True), first.shape)
+            for j in range(8)
+        ]
+        panel = jnp.where(inner, jnp.where(lane - k0 == sub, 1.0, 0.0), first)
+        for j in range(8):
+            pivot = cols[j]
+            inv = 1.0 / pivot[:, j : j + 1, :]
+
+            def reduce_rows(x):
+                w = x[:, j : j + 1, :] * inv
+                return jnp.where(sub == j, w, x - pivot * w)
+
+            panel = reduce_rows(panel)
+            cols = [reduce_rows(x) if i > j else x for i, x in enumerate(cols)]
+        signed = jnp.where(lane < k0, -first, first)
+        keep = (iota((RANK, RANK), 1) < k0) | (iota((RANK, RANK), 1) >= k0 + 8)
+        for f in range(FOLDS):
+            a1, a2, a3 = pieces(signed[f])
+            b1, b2, b3 = pieces(panel[f])
+            lhs = jnp.concatenate([a1, a1, a2, a2, a1, a3, jnp.zeros((80, RANK), jnp.float32)], axis=0).T
+            rhs = jnp.concatenate([b1, b2, b1, b2, b3, b1, jnp.zeros((80, RANK), jnp.float32)], axis=0)
+            change = dot(lhs.astype(jnp.bfloat16), rhs.astype(jnp.bfloat16))
+            gram[f] = jnp.where(keep, gram[f], 0.0) - change
+        gram[:, pl.ds(k0, 8), :] = panel
+
+        r = pl.ds(pl.multiple_of(b * tall, tall), tall)
         byte = dot(lw[r, WIDE : WIDE + 128], expand).astype(jnp.int32)
-        bit = lax.shift_right_logical(byte, iota((128, width), 1) % 8) & 1
+        bit = lax.shift_right_logical(byte, mod(iota((tall, width), 1), 8)) & 1
         flag = bit.astype(jnp.float32).astype(jnp.bfloat16)
         kind[r, :] = jnp.concatenate([fw[r, :]] * (width // 128), axis=1) * flag
+
+        f = b // (steps // FOLDS)
+        q = pl.ds(pl.multiple_of(lax.rem(b, steps // FOLDS) * quarter, quarter), quarter)
+        left_f = lw[q, pl.ds(pl.multiple_of(f * RANK, RANK), RANK)]
+        pred[f, q, :] = dot(left_f, right[f], NT).astype(jnp.bfloat16)
         return carry
-
-    lax.fori_loop(0, WIN // 128, masks, 0)
 
     def collect(at):
         swap_recv(*datas[at])
         cols = slice(at * part, (at + 1) * part)
 
-        def gather(t, carry):
-            r = pl.ds(pl.multiple_of(t * 128, 128), 128)
-            dw[r, cols] = dot(umat[r, :], got[:, :, cols].reshape(CORE, part)).astype(jnp.bfloat16)
-            return carry
-
-        dpack[:, cols] = dot(umat[CORE : CORE + PACK, :], got[:, :, cols].reshape(CORE, part)).astype(jnp.bfloat16)
-        lax.fori_loop(0, CORE // 128, gather, 0)
+        arrived = got[:, :, cols].reshape(CORE, part)
+        dpack[:, cols] = dot(umat[CORE : CORE + PACK, :], arrived).astype(jnp.bfloat16)
+        dw[0:CORE, cols] = dot(umat[0:CORE, :], arrived).astype(jnp.bfloat16)
         halo_start(*halos[at])
 
     def finish(at):
@@ -421,16 +434,9 @@
         swap_recv(*rets[at])
         out[:, cols] = dot(qmat[...], ret[:, :, cols].reshape(CORE, part)).astype(jnp.bfloat16)
 
+    lax.fori_loop(0, steps // 2, eliminate, 0)
     collect(0)
-
-    for f in range(FOLDS):
-        def predict(t, carry, f=f):
-            r = pl.ds(pl.multiple_of(t * 128, 128), 128)
-            pred[f, r, :] = dot(lw[r, f * RANK : (f + 1) * RANK], right[f], NT).astype(jnp.bfloat16)
-            return carry
-
-        lax.fori_loop(0, WIN // 128, predict, 0)
-
+    lax.fori_loop(steps // 2, steps, eliminate, 0)
     collect(1)
     for at in range(PARTS):
         finish(at)
@@ -494,7 +500,7 @@
             pltpu.VMEM((CORE, CORE), bf),
             pltpu.VMEM((CORE, CORE), bf),
             pltpu.VMEM((CORE, WIDE), bf),
-            dma((1, peers)), dma((1, peers)), dma((PARTS, peers)), dma((PARTS, peers)), dma((PARTS, peers)), dma((PARTS, peers)),
+            dma((1,)), dma((1,)), dma((PARTS,)), dma((PARTS,)), dma((PARTS,)), dma((PARTS,)),
             dma((1, 8)), dma((1, 8)), dma((1, 8)), dma((1, 8)), dma((PARTS, 8)), dma((PARTS, 8)),
         ],
         compiler_params=pltpu.CompilerParams(

time: 96.5 us -> 88.4 us (0.916)
  Pallas kernels: 88.4 us -> 80.3 us
    pallas_call x1, Pallas kernels: 88.4 us -> 80.3 us  [fused(): pl.pallas_call(functools.partial(kernel, n_long, n_short), out_shape=(jax...]
where the time goes in v2:
time: 88.4 us; the launch traced here: 88.2 us
  Pallas kernels  80.3 us (91%)
  local copies, waits for them, and re-layouts  6.26 us (7%)
  other arithmetic  1 us (1%)
    pallas_call x1, Pallas kernels, fused(): pl.pallas_call(functools.partial(kernel, n_long, n_short), out_shape=(jax...  80.3 us
    unnamed x6, local copies, waits for them, and re-layouts  6.26 us

profile of v2, /device:TPU:0, one launch (start us, length us, event | category | flops | bytes accessed | tf_op | source)
XLA Modules:
  0.0 88.2 jit_solution(8209618021512270475)
XLA Ops:
  0.6 1.0 %copy.11 = s32[512,64]{1,0:T(8,128)S(1)} copy(s32[512,64]{0,1:T(8,128)} %param.11) | data formatting | bytes 262144 | tf_op args[4]
  1.7 0.1 and_convert_fusion
  1.7 1.1 %copy.17 = bf16[64,8,4,128]{3,1,2,0:T(8,128)(2,1)S(1)} copy(bf16[64,8,4,128]{3,2,1,0:T(4,128)(2,1)} %bitcast.8) | data formatting | bytes 1048576
  2.9 0.9 %pad_maximum_fusion.side = bf16[512,640]{1,0:T(8,128)(2,1)} fusion(bf16[512,64]{1,0:T(8,128)(2,1)S(1)} %get-tuple-element.3, bf16[512,64]{1,0:T(8,128)(2,1)S(1)} %get-tuple-element.2, bf16[512,512]{1,0:T(8,128)(2,1)S(1)} %bitcast.7), kind=kLoop, calls=%fused_computation | loop fusion | flops 1966080 | bytes 1310720 | tf_op jit(solution)/shard_map/concatenate | solution.py:469
  3.8 80.3 %shard_map.86 = (f32[4,1024,128]{2,1,0:T(8,128)}, bf16[512,1024]{1,0:T(8,128)(2,1)}) custom-call(bf16[512,1024]{1,0:T(8,128)(2,1)} %traces.1, s32[1,512]{1,0:T(1,128)} %bitcast.9, s32[1,512]{1,0:T(1,128)} %bitcast.10, s32[1,512]{1,0:T(1,128)} %bitcast.11, bf16[512,640]{1,0:T(8,128)(2,1)} %pad_maximum_fusion.side, bf16[4,1024,128]{2,1,0:T(8,128)(2,1)} %right.1), custom_call_target="tpu_custom_call" | custom-call | tf_op jit(solution)/shard_map/pallas_call | solution.py:473
  84.1 0.0 copy-start
  84.1 3.1 %copy.20 = f32[4,1024,128]{2,1,0:T(8,128)} copy(f32[4,1024,128]{2,1,0:T(8,128)} %get-tuple-element.6) | data formatting | bytes 4194304
  87.2 0.0 copy-done
  87.2 1.0 %copy.21 = bf16[512,1024]{1,0:T(8,128)(2,1)} copy(bf16[512,1024]{1,0:T(8,128)(2,1)S(1)} %copy-done) | data formatting | bytes 2097152
Async XLA Ops:
  84.1 3.1 %copy-start = (bf16[512,1024]{1,0:T(8,128)(2,1)S(1)}, bf16[512,1024]{1,0:T(8,128)(2,1)}, u32[]{:S(2)}) copy-start(bf16[512,1024]{1,0:T(8,128)(2,1)} %get-tuple-element.7) | copy-start | bytes 3145732

commit v3 on v2

--- a/solution.py
+++ b/solution.py
@@ -131,7 +131,7 @@
 WIN = 1024
 CORE = CX * CY
 WIDE = FOLDS * RANK
-PARTS = 4
+PARTS = 2
 NT = (((1,), (1,)), ((), ()))
 HALO = (
     (1, 0, False, CORE - H * CY, CORE, H * CY),
@@ -204,12 +204,11 @@
 
     barrier = pltpu.get_barrier_semaphore()
 
-    def greet(k, carry):
+    others = [None]
+    for k in range(1, peers):
         q = lax.rem(me + k, peers)
-        pl.semaphore_signal(barrier, inc=1, device_id=(q // n_short, lax.rem(q, n_short)), device_id_type=MESH)
-        return carry
-
-    lax.fori_loop(1, peers, greet, 0)
+        others.append((q, (q // n_short, lax.rem(q, n_short))))
+        pl.semaphore_signal(barrier, inc=1, device_id=others[k][1], device_id_type=MESH)
 
     owner = own[...]
     oh = flags(iota((peers, CORE), 0) == owner, jnp.float32)
@@ -262,13 +261,13 @@
                 halo(*refs, i).wait_send()
 
     def swap(src, dst, send_sem, recv_sem, at, span, k):
-        to = lax.rem(me + k, peers)
+        to, place_of_to = others[k]
         return pltpu.make_async_remote_copy(
             src_ref=src.at[to, :, pl.ds(at * span, span)],
             dst_ref=dst.at[me, :, pl.ds(at * span, span)],
             send_sem=send_sem.at[at],
             recv_sem=recv_sem.at[at],
-            device_id=(to // n_short, lax.rem(to, n_short)),
+            device_id=place_of_to,
             device_id_type=MESH,
         )
 
@@ -283,11 +282,8 @@
         )
 
     def swap_start(*refs):
-        def go(k, carry):
+        for k in range(1, peers):
             swap(*refs, k).start()
-            return carry
-
-        lax.fori_loop(1, peers, go, 0)
 
     def swap_recv(*refs):
         all_of(*refs).wait_recv()
@@ -504,7 +500,7 @@
             dma((1, 8)), dma((1, 8)), dma((1, 8)), dma((1, 8)), dma((PARTS, 8)), dma((PARTS, 8)),
         ],
         compiler_params=pltpu.CompilerParams(
-            collective_id=0, has_side_effects=True, vmem_limit_bytes=56 * 1024 * 1024
+            collective_id=0, has_side_effects=True, vmem_limit_bytes=44 * 1024 * 1024
         ),
     )(
         acq_traces, route_owner.reshape(1, rows), route_row.reshape(1, rows), route_fold.reshape(1, rows),

time: 88.4 us -> 80.3 us (0.908)
  Pallas kernels: 80.3 us -> 74.4 us
  local copies, waits for them, and re-layouts: 6.26 us -> 4.85 us
    pallas_call x1, Pallas kernels: 80.3 us -> 74.4 us  [fused(): pl.pallas_call(functools.partial(kernel, n_long, n_short), out_shape=(jax...]
    unnamed x6 -> x14, local copies, waits for them, and re-layouts: 6.26 us -> 4.85 us
where the time goes in v3:
time: 80.3 us; the launch traced here: 80.1 us
  Pallas kernels  74.4 us (93%)
  local copies, waits for them, and re-layouts  4.85 us (6%)
    pallas_call x1, Pallas kernels, fused(): pl.pallas_call(functools.partial(kernel, n_long, n_short), out_shape=(jax...  74.4 us
    unnamed x14, local copies, waits for them, and re-layouts  4.85 us

profile of v3, /device:TPU:0, one launch (start us, length us, event | category | flops | bytes accessed | tf_op | source)
XLA Modules:
  0.0 80.1 jit_solution(11855121734160634235)
XLA Ops:
  0.6 1.0 %copy.11 = s32[512,64]{1,0:T(8,128)S(1)} copy(s32[512,64]{0,1:T(8,128)} %param.11) | data formatting | bytes 262144 | tf_op args[4]
  1.7 0.1 and_convert_fusion
  1.7 0.0 copy-start
  1.7 0.0 copy-start.1
  1.8 0.0 copy-start.2
  1.8 0.0 copy-start.3
  1.8 0.0 copy-start.4
  1.8 1.3 %copy.17 = bf16[64,8,4,128]{3,1,2,0:T(8,128)(2,1)S(1)} copy(bf16[64,8,4,128]{3,2,1,0:T(4,128)(2,1)} %bitcast.11) | data formatting | bytes 1048576
  3.1 0.1 pad_maximum_fusion.side
  3.2 0.0 copy-done
  3.2 0.2 copy-done.1
  3.4 0.0 copy-done.2
  3.4 0.0 copy-done.3
  3.4 0.0 copy-done.4
  3.4 74.4 %shard_map.86 = (f32[4,1024,128]{2,1,0:T(8,128)S(1)}, bf16[512,1024]{1,0:T(8,128)(2,1)S(1)}) custom-call(bf16[512,1024]{1,0:T(8,128)(2,1)S(1)} %copy-done, s32[1,512]{1,0:T(1,128)S(1)} %bitcast.7, s32[1,512]{1,0:T(1,128)S(1)} %bitcast.8, s32[1,512]{1,0:T(1,128)S(1)} %bitcast.9, bf16[512,640]{1,0:T(8,128)(2,1)S(1)} %pad_maximum_fusion.side, ...), custom_call_target="tpu_custom_call" | custom-call | tf_op jit(solution)/shard_map/pallas_call | solution.py:469
  77.8 1.3 %copy.20 = f32[4,1024,128]{2,1,0:T(8,128)} copy(f32[4,1024,128]{2,1,0:T(8,128)S(1)} %get-tuple-element.6) | data formatting | bytes 4194304
  79.2 1.0 %copy.21 = bf16[512,1024]{1,0:T(8,128)(2,1)} copy(bf16[512,1024]{1,0:T(8,128)(2,1)S(1)} %get-tuple-element.7) | data formatting | bytes 2097152
Async XLA Ops:
  1.7 1.4 %copy-start = (bf16[512,1024]{1,0:T(8,128)(2,1)S(1)}, bf16[512,1024]{1,0:T(8,128)(2,1)}, u32[]{:S(2)}) copy-start(bf16[512,1024]{1,0:T(8,128)(2,1)} %traces.1) | copy-start | bytes 3145732
  1.7 1.7 %copy-start.1 = (bf16[4,1024,128]{2,1,0:T(8,128)(2,1)S(1)}, bf16[4,1024,128]{2,1,0:T(8,128)(2,1)}, u32[]{:S(2)}) copy-start(bf16[4,1024,128]{2,1,0:T(8,128)(2,1)} %right.1) | copy-start | bytes 3145732
  1.8 1.7 %copy-start.2 = (s32[512]{0:T(512)S(1)}, s32[512]{0:T(512)}, u32[]{:S(2)}) copy-start(s32[512]{0:T(512)} %param.8) | copy-start | bytes 6148
  1.8 1.7 %copy-start.3 = (s32[512]{0:T(512)S(1)}, s32[512]{0:T(512)}, u32[]{:S(2)}) copy-start(s32[512]{0:T(512)} %param.9) | copy-start | bytes 6148
  1.8 1.7 %copy-start.4 = (s32[512]{0:T(512)S(1)}, s32[512]{0:T(512)}, u32[]{:S(2)}) copy-start(s32[512]{0:T(512)} %param.10) | copy-start | bytes 6148

commit v4 on v3

--- a/solution.py
+++ b/solution.py
@@ -186,7 +186,7 @@
 
 def kernel(
     n_long, n_short, traces, own, row, fold, side, right, news, out,
-    lw, lpack, fw, fpack, dw, dpack, meta_out, meta_in, send, got, ret, back, pred, kind, cross, lt, gram, umat, vmat, qmat, csel,
+    lw, lpack, fw, fpack, dw, dpack, meta_out, meta_in, send, got, ret, back, kind, cross, lt, ltm, gram, umat, vmat, qmat, csel,
     meta_s, meta_r, data_s, data_r, ret_s, ret_r, hl_s, hl_r, hf_s, hf_r, hd_s, hd_r,
 ):
     peers = n_long * n_short
@@ -326,10 +326,9 @@
         lines.append(jnp.sum(jnp.where(mine, dot(meta_got, place_of), 0.0), axis=0, keepdims=True))
     got_row = jnp.where(lines[2] > 0.5, lines[0] * 128.0 + lines[1], -1.0).astype(jnp.int32)
     got_fold = jnp.broadcast_to(lines[2], (128, CORE)).astype(jnp.bfloat16)
-    umat[0:CORE, :] = flags(iota((CORE, CORE), 0) == got_row)
-    umat[CORE : CORE + PACK, :] = flags(packed_rows((PACK, CORE)) == got_row)
-    fw[0:CORE, :] = dot(umat[0:CORE, :], got_fold, NT).astype(jnp.bfloat16)
-    fpack[...] = dot(umat[CORE : CORE + PACK, :], got_fold, NT).astype(jnp.bfloat16)
+    umat[...] = flags(iota((CORE, CORE), 0) == got_row)
+    fw[0:CORE, :] = dot(umat[...], got_fold, NT).astype(jnp.bfloat16)
+    fpack[...] = dot(pick, fw[0:CORE, :]).astype(jnp.bfloat16)
     halo_start(*folds)
     vmat[...] = flags(column(got_row) == iota((CORE, CORE), 1))
     for f in range(FOLDS):
@@ -349,7 +348,22 @@
     expand = flags(words == div(offs, 16) + jnp.where(mod(offs, 16) >= 8, 64, 0))
     steps = RANK // 8
     tall = WIN // steps
-    quarter = FOLDS * WIN // steps
+
+    cross[...] = jnp.zeros_like(cross)
+    sorts = fw[...].astype(jnp.float32)
+    for f in range(FOLDS):
+        kept = jnp.where((sorts > 0.5) & (sorts != f + 1.0), lw[:, f * RANK : (f + 1) * RANK].astype(jnp.float32), 0.0)
+        ltm[f * RANK : (f + 1) * RANK, :] = kept.astype(jnp.bfloat16).T
+
+    def classify(start, count):
+        r = pl.ds(start, count)
+        byte = dot(lw[r, WIDE : WIDE + 128], expand).astype(jnp.int32)
+        bit = lax.shift_right_logical(byte, mod(iota((count, width), 1), 8)) & 1
+        flag = bit.astype(jnp.float32).astype(jnp.bfloat16)
+        kind[r, :] = jnp.concatenate([fw[r, :]] * (width // 128), axis=1) * flag
+
+    quarter = WIN // FOLDS
+    classify(0, quarter)
 
     def eliminate(b, carry):
         k0 = pl.multiple_of(b * 8, 8)
@@ -383,16 +397,16 @@
             gram[f] = jnp.where(keep, gram[f], 0.0) - change
         gram[:, pl.ds(k0, 8), :] = panel
 
-        r = pl.ds(pl.multiple_of(b * tall, tall), tall)
-        byte = dot(lw[r, WIDE : WIDE + 128], expand).astype(jnp.int32)
-        bit = lax.shift_right_logical(byte, mod(iota((tall, width), 1), 8)) & 1
-        flag = bit.astype(jnp.float32).astype(jnp.bfloat16)
-        kind[r, :] = jnp.concatenate([fw[r, :]] * (width // 128), axis=1) * flag
-
-        f = b // (steps // FOLDS)
-        q = pl.ds(pl.multiple_of(lax.rem(b, steps // FOLDS) * quarter, quarter), quarter)
-        left_f = lw[q, pl.ds(pl.multiple_of(f * RANK, RANK), RANK)]
-        pred[f, q, :] = dot(left_f, right[f], NT).astype(jnp.bfloat16)
+        f = lax.rem(b, FOLDS)
+        q = pl.multiple_of(b // FOLDS * quarter, quarter)
+        r = pl.ds(q, quarter)
+        sort = kind[r, :]
+        left_f = lw[r, pl.ds(pl.multiple_of(f * RANK, RANK), RANK)]
+        guess = dot(left_f, right[f], NT).astype(jnp.bfloat16)
+        train = (sort > 0.5) & (sort != (f + 1).astype(jnp.bfloat16))
+        missing = jnp.where(train, jnp.zeros_like(guess), guess)
+        cross[f] += dot(lt[f, :, r], missing)
+        classify(pl.multiple_of(lax.rem(b + FOLDS, steps) * tall, tall), tall)
         return carry
 
     def collect(at):
@@ -400,20 +414,23 @@
         cols = slice(at * part, (at + 1) * part)
 
         arrived = got[:, :, cols].reshape(CORE, part)
-        dpack[:, cols] = dot(umat[CORE : CORE + PACK, :], arrived).astype(jnp.bfloat16)
-        dw[0:CORE, cols] = dot(umat[0:CORE, :], arrived).astype(jnp.bfloat16)
+        present = kind[0:CORE, cols].astype(jnp.float32) > 0.5
+        dw[0:CORE, cols] = jnp.where(present, dot(umat[...], arrived), 0.0).astype(jnp.bfloat16)
+        dpack[:, cols] = dot(pick, dw[0:CORE, cols]).astype(jnp.bfloat16)
         halo_start(*halos[at])
 
     def finish(at):
         cols = slice(at * part, (at + 1) * part)
         halo_recv(*halos[at])
+        known = dot(ltm[...], dw[:, cols])
         newb = []
         for f in range(FOLDS):
-            sort = kind[:, cols]
-            train = (sort > 0.5) & (sort != f + 1.0)
-            filled = jnp.where(train, dw[:, cols], pred[f, :, cols])
-            total = dot(lt[f], filled)
-            update = dot(gram[f], total, precision=lax.Precision.HIGHEST)
+            total = known[f * RANK : (f + 1) * RANK, :] + cross[f, :, cols]
+            a1, a2, a3 = pieces(gram[f])
+            b1, b2, b3 = pieces(total)
+            lhs = jnp.concatenate([a1, a1, a2, a2, a1, a3], axis=1).astype(jnp.bfloat16)
+            rhs = jnp.concatenate([b1, b2, b1, b2, b3, b1], axis=0).astype(jnp.bfloat16)
+            update = dot(lhs, rhs)
             cross[f, :, cols] = update
             newb.append(update.astype(jnp.bfloat16))
         chosen = dot(csel[...], jnp.concatenate(newb, axis=0))
@@ -487,12 +504,12 @@
             pltpu.VMEM((peers, cap, width), bf),
             pltpu.VMEM((peers, cap, width), bf),
             pltpu.VMEM((peers, cap, width), bf),
-            pltpu.VMEM((FOLDS, WIN, width), bf),
             pltpu.VMEM((WIN, width), bf),
             pltpu.VMEM((FOLDS, RANK, width), jnp.float32),
             pltpu.VMEM((FOLDS, RANK, WIN), bf),
+            pltpu.VMEM((WIDE, WIN), bf),
             pltpu.VMEM((FOLDS, RANK, RANK), jnp.float32),
-            pltpu.VMEM((CORE + PACK, CORE), bf),
+            pltpu.VMEM((CORE, CORE), bf),
             pltpu.VMEM((CORE, CORE), bf),
             pltpu.VMEM((CORE, CORE), bf),
             pltpu.VMEM((CORE, WIDE), bf),
@@ -500,7 +517,7 @@
             dma((1, 8)), dma((1, 8)), dma((1, 8)), dma((1, 8)), dma((PARTS, 8)), dma((PARTS, 8)),
         ],
         compiler_params=pltpu.CompilerParams(
-            collective_id=0, has_side_effects=True, vmem_limit_bytes=44 * 1024 * 1024
+            collective_id=0, has_side_effects=True, vmem_limit_bytes=40 * 1024 * 1024
         ),
     )(
         acq_traces, route_owner.reshape(1, rows), route_row.reshape(1, rows), route_fold.reshape(1, rows),

time: 80.3 us -> 83.5 us (1.040)
  Pallas kernels: 74.4 us -> 77.6 us
    pallas_call x1, Pallas kernels: 74.4 us -> 77.6 us  [fused(): pl.pallas_call(functools.partial(kernel, n_long, n_short), out_shape=(jax...]
where the time goes in v4:
time: 83.5 us; the launch traced here: 83.3 us
  Pallas kernels  77.6 us (93%)
  local copies, waits for them, and re-layouts  4.85 us (6%)
    pallas_call x1, Pallas kernels, fused(): pl.pallas_call(functools.partial(kernel, n_long, n_short), out_shape=(jax...  77.6 us
    unnamed x14, local copies, waits for them, and re-layouts  4.85 us

profile of v4, /device:TPU:0, one launch (start us, length us, event | category | flops | bytes accessed | tf_op | source)
XLA Modules:
  0.0 83.3 jit_solution(12942885221481924958)
XLA Ops:
  0.6 1.0 %copy.11 = s32[512,64]{1,0:T(8,128)S(1)} copy(s32[512,64]{0,1:T(8,128)} %param.11) | data formatting | bytes 262144 | tf_op args[4]
  1.7 0.1 and_convert_fusion
  1.7 0.0 copy-start
  1.7 0.0 copy-start.1
  1.8 0.0 copy-start.2
  1.8 0.0 copy-start.3
  1.8 0.0 copy-start.4
  1.8 1.3 %copy.17 = bf16[64,8,4,128]{3,1,2,0:T(8,128)(2,1)S(1)} copy(bf16[64,8,4,128]{3,2,1,0:T(4,128)(2,1)} %bitcast.11) | data formatting | bytes 1048576
  3.1 0.1 pad_maximum_fusion.side
  3.2 0.0 copy-done
  3.2 0.2 copy-done.1
  3.4 0.0 copy-done.2
  3.4 0.0 copy-done.3
  3.4 0.0 copy-done.4
  3.4 77.6 %shard_map.86 = (f32[4,1024,128]{2,1,0:T(8,128)S(1)}, bf16[512,1024]{1,0:T(8,128)(2,1)S(1)}) custom-call(bf16[512,1024]{1,0:T(8,128)(2,1)S(1)} %copy-done, s32[1,512]{1,0:T(1,128)S(1)} %bitcast.7, s32[1,512]{1,0:T(1,128)S(1)} %bitcast.8, s32[1,512]{1,0:T(1,128)S(1)} %bitcast.9, bf16[512,640]{1,0:T(8,128)(2,1)S(1)} %pad_maximum_fusion.side, ...), custom_call_target="tpu_custom_call" | custom-call | tf_op jit(solution)/shard_map/pallas_call | solution.py:486
  81.0 1.3 %copy.20 = f32[4,1024,128]{2,1,0:T(8,128)} copy(f32[4,1024,128]{2,1,0:T(8,128)S(1)} %get-tuple-element.6) | data formatting | bytes 4194304
  82.3 1.0 %copy.21 = bf16[512,1024]{1,0:T(8,128)(2,1)} copy(bf16[512,1024]{1,0:T(8,128)(2,1)S(1)} %get-tuple-element.7) | data formatting | bytes 2097152
Async XLA Ops:
  1.7 1.4 %copy-start = (bf16[512,1024]{1,0:T(8,128)(2,1)S(1)}, bf16[512,1024]{1,0:T(8,128)(2,1)}, u32[]{:S(2)}) copy-start(bf16[512,1024]{1,0:T(8,128)(2,1)} %traces.1) | copy-start | bytes 3145732
  1.7 1.7 %copy-start.1 = (bf16[4,1024,128]{2,1,0:T(8,128)(2,1)S(1)}, bf16[4,1024,128]{2,1,0:T(8,128)(2,1)}, u32[]{:S(2)}) copy-start(bf16[4,1024,128]{2,1,0:T(8,128)(2,1)} %right.1) | copy-start | bytes 3145732
  1.8 1.7 %copy-start.2 = (s32[512]{0:T(512)S(1)}, s32[512]{0:T(512)}, u32[]{:S(2)}) copy-start(s32[512]{0:T(512)} %param.8) | copy-start | bytes 6148
  1.8 1.7 %copy-start.3 = (s32[512]{0:T(512)S(1)}, s32[512]{0:T(512)}, u32[]{:S(2)}) copy-start(s32[512]{0:T(512)} %param.9) | copy-start | bytes 6148
  1.8 1.7 %copy-start.4 = (s32[512]{0:T(512)S(1)}, s32[512]{0:T(512)}, u32[]{:S(2)}) copy-start(s32[512]{0:T(512)} %param.10) | copy-start | bytes 6148

commit v5 on v4

--- a/solution.py
+++ b/solution.py
@@ -186,7 +186,7 @@
 
 def kernel(
     n_long, n_short, traces, own, row, fold, side, right, news, out,
-    lw, lpack, fw, fpack, dw, dpack, meta_out, meta_in, send, got, ret, back, kind, cross, lt, ltm, gram, umat, vmat, qmat, csel,
+    lw, lpack, fw, fpack, dw, dpack, meta_out, meta_in, send, got, ret, back, kind, cross, lt, ltm, gram, umat, vmat, qmat, csel, expand,
     meta_s, meta_r, data_s, data_r, ret_s, ret_r, hl_s, hl_r, hf_s, hf_r, hd_s, hd_r,
 ):
     peers = n_long * n_short
@@ -345,25 +345,27 @@
     halo_recv(*folds)
     words = iota((128, width), 0)
     offs = iota((128, width), 1)
-    expand = flags(words == div(offs, 16) + jnp.where(mod(offs, 16) >= 8, 64, 0))
+    expand[...] = flags(words == div(offs, 16) + jnp.where(mod(offs, 16) >= 8, 64, 0))
     steps = RANK // 8
-    tall = WIN // steps
-
-    cross[...] = jnp.zeros_like(cross)
-    sorts = fw[...].astype(jnp.float32)
+
+    sorts = fw[...].T.astype(jnp.float32)
     for f in range(FOLDS):
-        kept = jnp.where((sorts > 0.5) & (sorts != f + 1.0), lw[:, f * RANK : (f + 1) * RANK].astype(jnp.float32), 0.0)
-        ltm[f * RANK : (f + 1) * RANK, :] = kept.astype(jnp.bfloat16).T
-
-    def classify(start, count):
-        r = pl.ds(start, count)
-        byte = dot(lw[r, WIDE : WIDE + 128], expand).astype(jnp.int32)
-        bit = lax.shift_right_logical(byte, mod(iota((count, width), 1), 8)) & 1
-        flag = bit.astype(jnp.float32).astype(jnp.bfloat16)
-        kind[r, :] = jnp.concatenate([fw[r, :]] * (width // 128), axis=1) * flag
-
-    quarter = WIN // FOLDS
-    classify(0, quarter)
+        kept = jnp.where((sorts > 0.5) & (sorts != f + 1.0), lt[f].astype(jnp.float32), 0.0)
+        ltm[f * RANK : (f + 1) * RANK, :] = kept.astype(jnp.bfloat16)
+
+    tall = WIN // FOLDS
+    quarter = width // FOLDS
+    shifts = mod(iota((tall, quarter), 1), 8)
+
+    def classify(start, q):
+        r = pl.ds(start, tall)
+        cols = pl.ds(q, quarter)
+        byte = dot(lw[r, WIDE : WIDE + 128], expand[:, cols]).astype(jnp.int32)
+        flag = (lax.shift_right_logical(byte, shifts) & 1).astype(jnp.float32).astype(jnp.bfloat16)
+        kind[r, cols] = jnp.concatenate([fw[r, :]] * (quarter // 128), axis=1) * flag
+
+    for i in range(FOLDS):
+        classify(i * tall, 0)
 
     def eliminate(b, carry):
         k0 = pl.multiple_of(b * 8, 8)
@@ -376,16 +378,20 @@
             for j in range(8)
         ]
         panel = jnp.where(inner, jnp.where(lane - k0 == sub, 1.0, 0.0), first)
-        for j in range(8):
-            pivot = cols[j]
-            inv = 1.0 / pivot[:, j : j + 1, :]
+        for j in range(0, 8, 2):
+            one, two = cols[j], cols[j + 1]
+            p, q = one[:, j : j + 1, :], two[:, j : j + 1, :]
+            r, t = one[:, j + 1 : j + 2, :], two[:, j + 1 : j + 2, :]
+            inv = 1.0 / (p * t - q * r)
+            p, q, r, t = p * inv, q * inv, r * inv, t * inv
 
             def reduce_rows(x):
-                w = x[:, j : j + 1, :] * inv
-                return jnp.where(sub == j, w, x - pivot * w)
+                u, v = x[:, j : j + 1, :], x[:, j + 1 : j + 2, :]
+                y, z = t * u - q * v, p * v - r * u
+                return jnp.where(sub == j, y, jnp.where(sub == j + 1, z, x - one * y - two * z))
 
             panel = reduce_rows(panel)
-            cols = [reduce_rows(x) if i > j else x for i, x in enumerate(cols)]
+            cols = [reduce_rows(x) if i > j + 1 else x for i, x in enumerate(cols)]
         signed = jnp.where(lane < k0, -first, first)
         keep = (iota((RANK, RANK), 1) < k0) | (iota((RANK, RANK), 1) >= k0 + 8)
         for f in range(FOLDS):
@@ -399,14 +405,15 @@
 
         f = lax.rem(b, FOLDS)
         q = pl.multiple_of(b // FOLDS * quarter, quarter)
-        r = pl.ds(q, quarter)
-        sort = kind[r, :]
-        left_f = lw[r, pl.ds(pl.multiple_of(f * RANK, RANK), RANK)]
-        guess = dot(left_f, right[f], NT).astype(jnp.bfloat16)
+        part_cols = pl.ds(q, quarter)
+        sort = kind[:, part_cols]
+        left_f = lw[:, pl.ds(pl.multiple_of(f * RANK, RANK), RANK)]
+        guess = dot(left_f, right[f, part_cols, :], NT).astype(jnp.bfloat16)
         train = (sort > 0.5) & (sort != (f + 1).astype(jnp.bfloat16))
         missing = jnp.where(train, jnp.zeros_like(guess), guess)
-        cross[f] += dot(lt[f, :, r], missing)
-        classify(pl.multiple_of(lax.rem(b + FOLDS, steps) * tall, tall), tall)
+        cross[f, :, part_cols] = dot(lt[f], missing)
+        ahead = lax.rem(b // FOLDS + 1, FOLDS)
+        classify(pl.multiple_of(f * tall, tall), pl.multiple_of(ahead * quarter, quarter))
         return carry
 
     def collect(at):
@@ -513,6 +520,7 @@
             pltpu.VMEM((CORE, CORE), bf),
             pltpu.VMEM((CORE, CORE), bf),
             pltpu.VMEM((CORE, WIDE), bf),
+            pltpu.VMEM((128, width), bf),
             dma((1,)), dma((1,)), dma((PARTS,)), dma((PARTS,)), dma((PARTS,)), dma((PARTS,)),
             dma((1, 8)), dma((1, 8)), dma((1, 8)), dma((1, 8)), dma((PARTS, 8)), dma((PARTS, 8)),
         ],

time: 83.5 us -> 84.3 us (level)
    pallas_call x1, Pallas kernels: 77.6 us -> 78.4 us  [fused(): pl.pallas_call(functools.partial(kernel, n_long, n_short), out_shape=(jax...]
where the time goes in v5:
time: 84.3 us; the launch traced here: 84.2 us
  Pallas kernels  78.4 us (93%)
  local copies, waits for them, and re-layouts  4.85 us (6%)
    pallas_call x1, Pallas kernels, fused(): pl.pallas_call(functools.partial(kernel, n_long, n_short), out_shape=(jax...  78.4 us
    unnamed x14, local copies, waits for them, and re-layouts  4.85 us

profile of v5, /device:TPU:0, one launch (start us, length us, event | category | flops | bytes accessed | tf_op | source)
XLA Modules:
  0.0 84.2 jit_solution(16214596802548437001)
XLA Ops:
  0.6 1.0 %copy.11 = s32[512,64]{1,0:T(8,128)S(1)} copy(s32[512,64]{0,1:T(8,128)} %param.11) | data formatting | bytes 262144 | tf_op args[4]
  1.7 0.1 and_convert_fusion
  1.7 0.0 copy-start
  1.7 0.0 copy-start.1
  1.8 0.0 copy-start.2
  1.8 0.0 copy-start.3
  1.8 0.0 copy-start.4
  1.8 1.3 %copy.17 = bf16[64,8,4,128]{3,1,2,0:T(8,128)(2,1)S(1)} copy(bf16[64,8,4,128]{3,2,1,0:T(4,128)(2,1)} %bitcast.11) | data formatting | bytes 1048576
  3.1 0.1 pad_maximum_fusion.side
  3.2 0.0 copy-done
  3.2 0.2 copy-done.1
  3.4 0.0 copy-done.2
  3.4 0.0 copy-done.3
  3.4 0.0 copy-done.4
  3.4 78.4 %shard_map.86 = (f32[4,1024,128]{2,1,0:T(8,128)S(1)}, bf16[512,1024]{1,0:T(8,128)(2,1)S(1)}) custom-call(bf16[512,1024]{1,0:T(8,128)(2,1)S(1)} %copy-done, s32[1,512]{1,0:T(1,128)S(1)} %bitcast.7, s32[1,512]{1,0:T(1,128)S(1)} %bitcast.8, s32[1,512]{1,0:T(1,128)S(1)} %bitcast.9, bf16[512,640]{1,0:T(8,128)(2,1)S(1)} %pad_maximum_fusion.side, ...), custom_call_target="tpu_custom_call" | custom-call | tf_op jit(solution)/shard_map/pallas_call | solution.py:493
  81.9 1.3 %copy.20 = f32[4,1024,128]{2,1,0:T(8,128)} copy(f32[4,1024,128]{2,1,0:T(8,128)S(1)} %get-tuple-element.6) | data formatting | bytes 4194304
  83.2 1.0 %copy.21 = bf16[512,1024]{1,0:T(8,128)(2,1)} copy(bf16[512,1024]{1,0:T(8,128)(2,1)S(1)} %get-tuple-element.7) | data formatting | bytes 2097152
Async XLA Ops:
  1.7 1.4 %copy-start = (bf16[512,1024]{1,0:T(8,128)(2,1)S(1)}, bf16[512,1024]{1,0:T(8,128)(2,1)}, u32[]{:S(2)}) copy-start(bf16[512,1024]{1,0:T(8,128)(2,1)} %traces.1) | copy-start | bytes 3145732
  1.7 1.7 %copy-start.1 = (bf16[4,1024,128]{2,1,0:T(8,128)(2,1)S(1)}, bf16[4,1024,128]{2,1,0:T(8,128)(2,1)}, u32[]{:S(2)}) copy-start(bf16[4,1024,128]{2,1,0:T(8,128)(2,1)} %right.1) | copy-start | bytes 3145732
  1.8 1.7 %copy-start.2 = (s32[512]{0:T(512)S(1)}, s32[512]{0:T(512)}, u32[]{:S(2)}) copy-start(s32[512]{0:T(512)} %param.8) | copy-start | bytes 6148
  1.8 1.7 %copy-start.3 = (s32[512]{0:T(512)S(1)}, s32[512]{0:T(512)}, u32[]{:S(2)}) copy-start(s32[512]{0:T(512)} %param.9) | copy-start | bytes 6148
  1.8 1.7 %copy-start.4 = (s32[512]{0:T(512)S(1)}, s32[512]{0:T(512)}, u32[]{:S(2)}) copy-start(s32[512]{0:T(512)} %param.10) | copy-start | bytes 6148

commit v6 on v3

--- a/solution.py
+++ b/solution.py
@@ -349,7 +349,7 @@
     expand = flags(words == div(offs, 16) + jnp.where(mod(offs, 16) >= 8, 64, 0))
     steps = RANK // 8
     tall = WIN // steps
-    quarter = FOLDS * WIN // steps
+    quarter = FOLDS * width // steps
 
     def eliminate(b, carry):
         k0 = pl.multiple_of(b * 8, 8)
@@ -362,16 +362,20 @@
             for j in range(8)
         ]
         panel = jnp.where(inner, jnp.where(lane - k0 == sub, 1.0, 0.0), first)
-        for j in range(8):
-            pivot = cols[j]
-            inv = 1.0 / pivot[:, j : j + 1, :]
+        for j in range(0, 8, 2):
+            one, two = cols[j], cols[j + 1]
+            p, q = one[:, j : j + 1, :], two[:, j : j + 1, :]
+            r, t = one[:, j + 1 : j + 2, :], two[:, j + 1 : j + 2, :]
+            inv = 1.0 / (p * t - q * r)
+            p, q, r, t = p * inv, q * inv, r * inv, t * inv
 
             def reduce_rows(x):
-                w = x[:, j : j + 1, :] * inv
-                return jnp.where(sub == j, w, x - pivot * w)
+                u, v = x[:, j : j + 1, :], x[:, j + 1 : j + 2, :]
+                y, z = t * u - q * v, p * v - r * u
+                return jnp.where(sub == j, y, jnp.where(sub == j + 1, z, x - one * y - two * z))
 
             panel = reduce_rows(panel)
-            cols = [reduce_rows(x) if i > j else x for i, x in enumerate(cols)]
+            cols = [reduce_rows(x) if i > j + 1 else x for i, x in enumerate(cols)]
         signed = jnp.where(lane < k0, -first, first)
         keep = (iota((RANK, RANK), 1) < k0) | (iota((RANK, RANK), 1) >= k0 + 8)
         for f in range(FOLDS):
@@ -391,8 +395,8 @@
 
         f = b // (steps // FOLDS)
         q = pl.ds(pl.multiple_of(lax.rem(b, steps // FOLDS) * quarter, quarter), quarter)
-        left_f = lw[q, pl.ds(pl.multiple_of(f * RANK, RANK), RANK)]
-        pred[f, q, :] = dot(left_f, right[f], NT).astype(jnp.bfloat16)
+        left_f = lw[:, pl.ds(pl.multiple_of(f * RANK, RANK), RANK)]
+        pred[f, :, q] = dot(left_f, right[f, q, :], NT).astype(jnp.bfloat16)
         return carry
 
     def collect(at):
@@ -430,9 +434,8 @@
         swap_recv(*rets[at])
         out[:, cols] = dot(qmat[...], ret[:, :, cols].reshape(CORE, part)).astype(jnp.bfloat16)
 
-    lax.fori_loop(0, steps // 2, eliminate, 0)
+    lax.fori_loop(0, steps, eliminate, 0)
     collect(0)
-    lax.fori_loop(steps // 2, steps, eliminate, 0)
     collect(1)
     for at in range(PARTS):
         finish(at)

time: 80.3 us -> 84.9 us (1.057)
  Pallas kernels: 74.4 us -> 79 us
    pallas_call x1, Pallas kernels: 74.4 us -> 79 us  [fused(): pl.pallas_call(functools.partial(kernel, n_long, n_short), out_shape=(jax...]
where the time goes in v6:
time: 84.9 us; the launch traced here: 84.8 us
  Pallas kernels  79 us (93%)
  local copies, waits for them, and re-layouts  4.85 us (6%)
    pallas_call x1, Pallas kernels, fused(): pl.pallas_call(functools.partial(kernel, n_long, n_short), out_shape=(jax...  79 us
    unnamed x14, local copies, waits for them, and re-layouts  4.85 us

profile of v6, /device:TPU:0, one launch (start us, length us, event | category | flops | bytes accessed | tf_op | source)
XLA Modules:
  0.0 84.8 jit_solution(12560481884287477882)
XLA Ops:
  0.6 1.0 %copy.11 = s32[512,64]{1,0:T(8,128)S(1)} copy(s32[512,64]{0,1:T(8,128)} %param.11) | data formatting | bytes 262144 | tf_op args[4]
  1.7 0.1 and_convert_fusion
  1.7 0.0 copy-start
  1.7 0.0 copy-start.1
  1.8 0.0 copy-start.2
  1.8 0.0 copy-start.3
  1.8 0.0 copy-start.4
  1.8 1.3 %copy.17 = bf16[64,8,4,128]{3,1,2,0:T(8,128)(2,1)S(1)} copy(bf16[64,8,4,128]{3,2,1,0:T(4,128)(2,1)} %bitcast.11) | data formatting | bytes 1048576
  3.1 0.1 pad_maximum_fusion.side
  3.2 0.0 copy-done
  3.2 0.2 copy-done.1
  3.4 0.0 copy-done.2
  3.4 0.0 copy-done.3
  3.4 0.0 copy-done.4
  3.4 79.0 %shard_map.86 = (f32[4,1024,128]{2,1,0:T(8,128)S(1)}, bf16[512,1024]{1,0:T(8,128)(2,1)S(1)}) custom-call(bf16[512,1024]{1,0:T(8,128)(2,1)S(1)} %copy-done, s32[1,512]{1,0:T(1,128)S(1)} %bitcast.7, s32[1,512]{1,0:T(1,128)S(1)} %bitcast.8, s32[1,512]{1,0:T(1,128)S(1)} %bitcast.9, bf16[512,640]{1,0:T(8,128)(2,1)S(1)} %pad_maximum_fusion.side, ...), custom_call_target="tpu_custom_call" | custom-call | tf_op jit(solution)/shard_map/pallas_call | solution.py:472
  82.5 1.3 %copy.20 = f32[4,1024,128]{2,1,0:T(8,128)} copy(f32[4,1024,128]{2,1,0:T(8,128)S(1)} %get-tuple-element.6) | data formatting | bytes 4194304
  83.8 1.0 %copy.21 = bf16[512,1024]{1,0:T(8,128)(2,1)} copy(bf16[512,1024]{1,0:T(8,128)(2,1)S(1)} %get-tuple-element.7) | data formatting | bytes 2097152
Async XLA Ops:
  1.7 1.4 %copy-start = (bf16[512,1024]{1,0:T(8,128)(2,1)S(1)}, bf16[512,1024]{1,0:T(8,128)(2,1)}, u32[]{:S(2)}) copy-start(bf16[512,1024]{1,0:T(8,128)(2,1)} %traces.1) | copy-start | bytes 3145732
  1.7 1.7 %copy-start.1 = (bf16[4,1024,128]{2,1,0:T(8,128)(2,1)S(1)}, bf16[4,1024,128]{2,1,0:T(8,128)(2,1)}, u32[]{:S(2)}) copy-start(bf16[4,1024,128]{2,1,0:T(8,128)(2,1)} %right.1) | copy-start | bytes 3145732
  1.8 1.7 %copy-start.2 = (s32[512]{0:T(512)S(1)}, s32[512]{0:T(512)}, u32[]{:S(2)}) copy-start(s32[512]{0:T(512)} %param.8) | copy-start | bytes 6148
  1.8 1.7 %copy-start.3 = (s32[512]{0:T(512)S(1)}, s32[512]{0:T(512)}, u32[]{:S(2)}) copy-start(s32[512]{0:T(512)} %param.9) | copy-start | bytes 6148
  1.8 1.7 %copy-start.4 = (s32[512]{0:T(512)S(1)}, s32[512]{0:T(512)}, u32[]{:S(2)}) copy-start(s32[512]{0:T(512)} %param.10) | copy-start | bytes 6148
